TPU v7x, 32 devices: a whole 2x2x4 slice. The times are simulated.
32 devices in a mesh: dp: 4 (over y, x), ctx: 8 (over z, core).
Axes of the slice: x: 2, y: 2, z: 4, core: 2. Of those that a mesh axis runs over, the one named last changes fastest.
Arguments:
- inputs: bfloat16 [3, 4, 512, 1088], P(None, 'dp', 'ctx'), may hold values from -54 to 54
- lengths: int32 [3, 4, 4], P(None, 'dp'), may hold values from 1 to 509, as said below
- ln1_scale: bfloat16 [1088], P('dp'), may hold values from 0.5 to 1.5
- ln1_bias: bfloat16 [1088], P('dp'), may hold values from -4 to 4
- w_qkv: bfloat16 [1088, 3264], P('ctx', 'dp'), may hold values from -0.1875 to 0.1875
- qv_bias: bfloat16 [2176], P('dp'), may hold values from -4 to 4
- w_out: bfloat16 [1088, 1088], P('ctx', 'dp'), may hold values from -0.5 to 0.5
- out_bias: bfloat16 [1088], P('dp'), may hold values from -4 to 4
- ln2_scale: bfloat16 [1088], P('dp'), may hold values from 0.5 to 1.5
- ln2_bias: bfloat16 [1088], P('dp'), may hold values from -4 to 4
- w_up: bfloat16 [1088, 4352], P('ctx', 'dp'), may hold values from -0.1875 to 0.1875
- up_bias: bfloat16 [4352], P('dp'), may hold values from -4 to 4
- w_down: bfloat16 [4352, 1088], P('ctx', 'dp'), may hold values from -0.09375 to 0.09375
- down_bias: bfloat16 [1088], P('dp'), may hold values from -4 to 4
- out_grad: bfloat16 [3, 4, 512, 1088], P(None, 'dp', 'ctx'), may hold values from -6 to 6
Outputs:
- block_out: bfloat16 [3, 4, 512, 1088], P(None, 'dp', 'ctx')
- input_grad: bfloat16 [3, 4, 512, 1088], P(None, 'dp', 'ctx')
- ln1_scale_grad: float32 [1088], P('dp')
- ln1_bias_grad: float32 [1088], P('dp')
- w_qkv_grad: float32 [1088, 3264], P('ctx', 'dp')
- qv_bias_grad: float32 [2176], P('dp')
- w_out_grad: float32 [1088, 1088], P('ctx', 'dp')
- out_bias_grad: float32 [1088], P('dp')
- ln2_scale_grad: float32 [1088], P('dp')
- ln2_bias_grad: float32 [1088], P('dp')
- w_up_grad: float32 [1088, 4352], P('ctx', 'dp')
- up_bias_grad: float32 [4352], P('dp')
- w_down_grad: float32 [4352, 1088], P('ctx', 'dp')
- down_bias_grad: float32 [1088], P('dp')
Inputs may be any that keep to these rules, and one draw needn't show every extreme that they name: The 4 lengths of each stream sum to 512.
All inputs are finite; a program needn't handle non-finite values.
Results may differ from a plain program's by a relative error of at most 0.02.
Values may be sent and summed in bfloat16 or wider, within the bound.
A program may use at most 192 MiB of HBM per device.

v0:
```python
import jax
import jax.numpy as jnp
from jax import lax
from jax.sharding import PartitionSpec as P

HEADS = 17
HEAD_DIM = 64


EPSILON = 1e-05
SCALE = 0.125
NEGATIVE = -1e30


def passed_along(block, axis, distance):
    devices = range(lax.axis_size(axis))
    route = [(i - distance, i) for i in devices if i - distance in devices]
    return lax.ppermute(block, axis, route)


def from_behind(value, axis, steps):
    count = lax.axis_size(axis)
    pairs = [(source, (source + steps) % count) for source in range(count)]
    return lax.ppermute(value, axis, pairs)


def layer_norm(values, scale, shift):
    row_mean = jnp.mean(values, axis=-1, keepdims=True)
    centered = values - row_mean
    variance = jnp.mean(centered * centered, axis=-1, keepdims=True)
    inverse = lax.rsqrt(variance + EPSILON)
    normal = centered * inverse
    return (normal * scale + shift, normal, inverse)


def norm_back(grad_normed, normal, inverse, scale):
    scaled = grad_normed * scale
    return inverse * (
        scaled
        - jnp.mean(scaled, axis=-1, keepdims=True)
        - normal * jnp.mean(scaled * normal, axis=-1, keepdims=True)
    )


def outer_sum(left, right):
    return lax.dot_general(
        left, right, (((0,), (0,)), ((), ())), preferred_element_type=jnp.float32
    )


def back_dot(gradient, weight):
    return lax.dot_general(
        gradient, weight, (((1,), (1,)), ((), ())), preferred_element_type=jnp.float32
    )


def split_heads(columns):
    return columns.reshape(columns.shape[0], HEADS, HEAD_DIM)


def join_heads(per_head):
    return jnp.transpose(per_head, (1, 0, 2)).reshape(per_head.shape[1], HEADS * HEAD_DIM)


def doc_numbers(positions, seq_ends):
    return jnp.sum((positions[:, None] >= seq_ends[None, :]).astype(jnp.int32), axis=1)


def visible_mask(query_pos, query_doc, source, rows_here, seq_ends):
    key_pos = source * rows_here + jnp.arange(rows_here, dtype=jnp.int32)
    key_doc = doc_numbers(key_pos, seq_ends)
    return (
        (key_doc[None, :] == query_doc[:, None])
        & (key_pos[None, :] <= query_pos[:, None])
        & (source >= 0)
    )


def gather_all(shards):
    (
        w_qkv,
        w_out,
        w_up,
        w_down,
        ln1_scale,
        ln1_bias,
        qv_bias,
        out_bias,
        ln2_scale,
        ln2_bias,
        up_bias,
        down_bias,
    ) = shards
    rows_full = (
        lax.all_gather(w_qkv, "dp", axis=1, tiled=True),
        lax.all_gather(w_out, "dp", axis=1, tiled=True),
        lax.all_gather(w_up, "dp", axis=1, tiled=True),
        lax.all_gather(w_down, "dp", axis=1, tiled=True),
        lax.all_gather(ln1_scale, "dp", axis=0, tiled=True),
        lax.all_gather(ln1_bias, "dp", axis=0, tiled=True),
        lax.all_gather(qv_bias, "dp", axis=0, tiled=True),
        lax.all_gather(out_bias, "dp", axis=0, tiled=True),
        lax.all_gather(ln2_scale, "dp", axis=0, tiled=True),
        lax.all_gather(ln2_bias, "dp", axis=0, tiled=True),
        lax.all_gather(up_bias, "dp", axis=0, tiled=True),
        lax.all_gather(down_bias, "dp", axis=0, tiled=True),
    )
    matrices = (
        lax.all_gather(rows_full[0], "ctx", axis=0, tiled=True),
        lax.all_gather(rows_full[1], "ctx", axis=0, tiled=True),
        lax.all_gather(rows_full[2], "ctx", axis=0, tiled=True),
        lax.all_gather(rows_full[3], "ctx", axis=0, tiled=True),
    )
    vectors = tuple((member.astype(jnp.float32) for member in rows_full[4:]))
    return (matrices, vectors)


def attend_block(queries, kv_block, allowed, softmax_state):
    maximum, denominator, numerator = softmax_state
    model_width = kv_block.shape[1] // 2
    key_heads = split_heads(kv_block[:, :model_width])
    value_heads = split_heads(kv_block[:, model_width:])
    scores = (
        jnp.einsum("qhd,khd->hqk", queries, key_heads, preferred_element_type=jnp.float32) * SCALE
    )
    scores = jnp.where(allowed[None], scores, NEGATIVE)
    new_maximum = jnp.maximum(maximum, jnp.max(scores, axis=-1))
    weights = jnp.exp(scores - new_maximum[..., None])
    factor = jnp.exp(maximum - new_maximum)
    denominator = denominator * factor + jnp.sum(weights, axis=-1)
    numerator = numerator * factor[..., None] + jnp.einsum(
        "hqk,khd->hqd",
        weights.astype(jnp.bfloat16),
        value_heads,
        preferred_element_type=jnp.float32,
    )
    return (new_maximum, denominator, numerator)


def forward_pass(tokens, seq_ends, gathered, ctx_index, ctx_size):
    (w_qkv, w_out, w_up, w_down), vectors = gathered
    ln1_scale, ln1_bias, qv_bias, out_bias, ln2_scale, ln2_bias, up_bias, down_bias = vectors
    rows_here, model_width = tokens.shape
    tokens32 = tokens.astype(jnp.float32)
    normed1, normal1, inverse1 = layer_norm(tokens32, ln1_scale, ln1_bias)
    normed1 = normed1.astype(jnp.bfloat16)
    qkv_bias = jnp.concatenate(
        [qv_bias[:model_width], jnp.zeros((model_width,), jnp.float32), qv_bias[model_width:]]
    )
    qkv = (jnp.dot(normed1, w_qkv, preferred_element_type=jnp.float32) + qkv_bias).astype(
        jnp.bfloat16
    )
    queries = split_heads(qkv[:, :model_width])
    kv_block = qkv[:, model_width:]
    query_pos = ctx_index * rows_here + jnp.arange(rows_here, dtype=jnp.int32)
    query_doc = doc_numbers(query_pos, seq_ends)
    softmax_state = (
        jnp.full((HEADS, rows_here), NEGATIVE, jnp.float32),
        jnp.zeros((HEADS, rows_here), jnp.float32),
        jnp.zeros((HEADS, rows_here, HEAD_DIM), jnp.float32),
    )
    softmax_state = attend_block(
        queries,
        kv_block,
        visible_mask(query_pos, query_doc, ctx_index, rows_here, seq_ends),
        softmax_state,
    )

    def cycle_turn(section_index, cycle_state):
        moving, inner_state = cycle_state
        moving = passed_along(moving, "ctx", 1)
        source = ctx_index - section_index
        allowed = visible_mask(query_pos, query_doc, source, rows_here, seq_ends)
        return (moving, attend_block(queries, moving, allowed, inner_state))

    moved, softmax_state = lax.fori_loop(1, ctx_size, cycle_turn, (kv_block, softmax_state))
    maximum, denominator, numerator = softmax_state
    log_total = maximum + jnp.log(denominator)
    attended32 = join_heads(numerator / denominator[..., None])
    attended = attended32.astype(jnp.bfloat16)
    residual = tokens32 + jnp.dot(attended, w_out, preferred_element_type=jnp.float32) + out_bias
    normed2, normal2, inverse2 = layer_norm(residual, ln2_scale, ln2_bias)
    normed2 = normed2.astype(jnp.bfloat16)
    gelu_input = jnp.dot(normed2, w_up, preferred_element_type=jnp.float32) + up_bias
    hidden = jax.nn.gelu(gelu_input).astype(jnp.bfloat16)
    block_out = (
        residual + jnp.dot(hidden, w_down, preferred_element_type=jnp.float32) + down_bias
    ).astype(jnp.bfloat16)
    kept_values = (
        normed1,
        normal1,
        inverse1,
        queries,
        kv_block,
        normed2,
        normal2,
        inverse2,
        gelu_input,
        hidden,
        attended,
        attended32,
        log_total,
        query_pos,
        query_doc,
    )
    return (block_out, kept_values)


def backward_pass(grad_out, kept_values, seq_ends, gathered, ctx_index, ctx_size):
    (w_qkv, w_out, w_up, w_down), vectors = gathered
    ln1_scale, ln1_bias, qv_bias, out_bias, ln2_scale, ln2_bias, up_bias, down_bias = vectors
    (
        normed1,
        normal1,
        inverse1,
        queries,
        kv_block,
        normed2,
        normal2,
        inverse2,
        gelu_input,
        hidden,
        attended,
        attended32,
        log_total,
        query_pos,
        query_doc,
    ) = kept_values
    rows_here, model_width = grad_out.shape
    grad32 = grad_out.astype(jnp.float32)
    grad_hidden = back_dot(grad_out, w_down)
    gelu_pull = jax.vjp(jax.nn.gelu, gelu_input)[1]
    grad_upper = gelu_pull(grad_hidden)[0].astype(jnp.bfloat16)
    grad_normed2 = back_dot(grad_upper, w_up)
    grad_residual = grad32 + norm_back(grad_normed2, normal2, inverse2, ln2_scale)
    grad_branch = grad_residual.astype(jnp.bfloat16)
    grad_attended = back_dot(grad_branch, w_out).astype(jnp.bfloat16)
    grad_heads = split_heads(grad_attended)
    row_dot = jnp.transpose(
        jnp.sum(split_heads(grad_attended.astype(jnp.float32) * attended32), axis=-1)
    )

    def grad_block(moving, allowed, grad_queries):
        key_heads = split_heads(moving[:, :model_width])
        value_heads = split_heads(moving[:, model_width:])
        scores = (
            jnp.einsum("qhd,khd->hqk", queries, key_heads, preferred_element_type=jnp.float32)
            * SCALE
        )
        scores = jnp.where(allowed[None], scores, NEGATIVE)
        weights = jnp.exp(scores - log_total[..., None])
        grad_weights = jnp.einsum(
            "qhd,khd->hqk", grad_heads, value_heads, preferred_element_type=jnp.float32
        )
        grad_scores = (weights * (grad_weights - row_dot[..., None])).astype(jnp.bfloat16)
        grad_queries = (
            grad_queries
            + jnp.einsum("hqk,khd->hqd", grad_scores, key_heads, preferred_element_type=jnp.float32)
            * SCALE
        )
        grad_keys = (
            jnp.einsum("hqk,qhd->khd", grad_scores, queries, preferred_element_type=jnp.float32)
            * SCALE
        )
        grad_values = jnp.einsum(
            "hqk,qhd->khd",
            weights.astype(jnp.bfloat16),
            grad_heads,
            preferred_element_type=jnp.float32,
        )
        kv_part = jnp.concatenate(
            [
                grad_keys.reshape(rows_here, model_width),
                grad_values.reshape(rows_here, model_width),
            ],
            axis=1,
        )
        return (grad_queries, kv_part)

    def back_turn(section_index, cycle_state):
        moving, grad_kv, grad_queries = cycle_state
        source = ctx_index - section_index
        allowed = visible_mask(query_pos, query_doc, source, rows_here, seq_ends)
        grad_queries, kv_part = grad_block(moving, allowed, grad_queries)
        grad_kv = from_behind((grad_kv + kv_part).astype(jnp.bfloat16), "ctx", 1).astype(
            jnp.float32
        )
        moving = passed_along(moving, "ctx", 1)
        return (moving, grad_kv, grad_queries)

    start_state = (
        kv_block,
        jnp.zeros((rows_here, 2 * model_width), jnp.float32),
        jnp.zeros((HEADS, rows_here, HEAD_DIM), jnp.float32),
    )
    moved, grad_kv, grad_queries = lax.fori_loop(0, ctx_size, back_turn, start_state)
    grad_qkv = jnp.concatenate([join_heads(grad_queries), grad_kv], axis=1).astype(jnp.bfloat16)
    grad_normed1 = back_dot(grad_qkv, w_qkv)
    input_grad = (grad_residual + norm_back(grad_normed1, normal1, inverse1, ln1_scale)).astype(
        jnp.bfloat16
    )
    qkv_wide = grad_qkv.astype(jnp.float32)
    gradients = (
        outer_sum(normed1, grad_qkv),
        outer_sum(attended, grad_branch),
        outer_sum(normed2, grad_upper),
        outer_sum(hidden, grad_out),
        jnp.sum(grad_normed1 * normal1, axis=0),
        jnp.sum(grad_normed1, axis=0),
        jnp.concatenate(
            [
                jnp.sum(qkv_wide[:, :model_width], axis=0),
                jnp.sum(qkv_wide[:, 2 * model_width :], axis=0),
            ]
        ),
        jnp.sum(grad_branch.astype(jnp.float32), axis=0),
        jnp.sum(grad_normed2 * normal2, axis=0),
        jnp.sum(grad_normed2, axis=0),
        jnp.sum(grad_upper.astype(jnp.float32), axis=0),
        jnp.sum(grad32, axis=0),
    )
    return (input_grad, gradients)


def local(
    inputs,
    lengths,
    ln1_scale,
    ln1_bias,
    w_qkv,
    qv_bias,
    w_out,
    out_bias,
    ln2_scale,
    ln2_bias,
    w_up,
    up_bias,
    w_down,
    down_bias,
    out_grad,
):
    ctx_index = lax.axis_index("ctx")
    ctx_size = lax.axis_size("ctx")
    shards = (
        w_qkv,
        w_out,
        w_up,
        w_down,
        ln1_scale,
        ln1_bias,
        qv_bias,
        out_bias,
        ln2_scale,
        ln2_bias,
        up_bias,
        down_bias,
    )
    gathered = None
    block_outs = []
    input_grads = []
    totals = None
    for micro_batch in range(inputs.shape[0]):
        seq_ends = jnp.cumsum(lengths[micro_batch, 0])
        gathered = gather_all(shards)
        block_out, kept_values = forward_pass(
            inputs[micro_batch, 0], seq_ends, gathered, ctx_index, ctx_size
        )
        gathered = gather_all(shards)
        input_grad, gradients = backward_pass(
            out_grad[micro_batch, 0], kept_values, seq_ends, gathered, ctx_index, ctx_size
        )
        block_outs.append(block_out)
        input_grads.append(input_grad)
        totals = gradients if totals is None else jax.tree.map(jnp.add, totals, gradients)
    row_parts = (
        lax.psum_scatter(
            totals[0].astype(jnp.bfloat16), "ctx", scatter_dimension=0, tiled=True
        ).astype(jnp.float32),
        lax.psum_scatter(
            totals[1].astype(jnp.bfloat16), "ctx", scatter_dimension=0, tiled=True
        ).astype(jnp.float32),
        lax.psum_scatter(
            totals[2].astype(jnp.bfloat16), "ctx", scatter_dimension=0, tiled=True
        ).astype(jnp.float32),
        lax.psum_scatter(
            totals[3].astype(jnp.bfloat16), "ctx", scatter_dimension=0, tiled=True
        ).astype(jnp.float32),
    )
    vector_totals = (
        lax.psum(totals[4].astype(jnp.bfloat16), "ctx").astype(jnp.float32),
        lax.psum(totals[5].astype(jnp.bfloat16), "ctx").astype(jnp.float32),
        lax.psum(totals[6].astype(jnp.bfloat16), "ctx").astype(jnp.float32),
        lax.psum(totals[7].astype(jnp.bfloat16), "ctx").astype(jnp.float32),
        lax.psum(totals[8].astype(jnp.bfloat16), "ctx").astype(jnp.float32),
        lax.psum(totals[9].astype(jnp.bfloat16), "ctx").astype(jnp.float32),
        lax.psum(totals[10].astype(jnp.bfloat16), "ctx").astype(jnp.float32),
        lax.psum(totals[11].astype(jnp.bfloat16), "ctx").astype(jnp.float32),
    )
    summed = (
        lax.psum_scatter(
            row_parts[0].astype(jnp.bfloat16), "dp", scatter_dimension=1, tiled=True
        ).astype(jnp.float32),
        lax.psum_scatter(
            row_parts[1].astype(jnp.bfloat16), "dp", scatter_dimension=1, tiled=True
        ).astype(jnp.float32),
        lax.psum_scatter(
            row_parts[2].astype(jnp.bfloat16), "dp", scatter_dimension=1, tiled=True
        ).astype(jnp.float32),
        lax.psum_scatter(
            row_parts[3].astype(jnp.bfloat16), "dp", scatter_dimension=1, tiled=True
        ).astype(jnp.float32),
        lax.psum_scatter(
            vector_totals[0].astype(jnp.bfloat16), "dp", scatter_dimension=0, tiled=True
        ).astype(jnp.float32),
        lax.psum_scatter(
            vector_totals[1].astype(jnp.bfloat16), "dp", scatter_dimension=0, tiled=True
        ).astype(jnp.float32),
        lax.psum_scatter(
            vector_totals[2].astype(jnp.bfloat16), "dp", scatter_dimension=0, tiled=True
        ).astype(jnp.float32),
        lax.psum_scatter(
            vector_totals[3].astype(jnp.bfloat16), "dp", scatter_dimension=0, tiled=True
        ).astype(jnp.float32),
        lax.psum_scatter(
            vector_totals[4].astype(jnp.bfloat16), "dp", scatter_dimension=0, tiled=True
        ).astype(jnp.float32),
        lax.psum_scatter(
            vector_totals[5].astype(jnp.bfloat16), "dp", scatter_dimension=0, tiled=True
        ).astype(jnp.float32),
        lax.psum_scatter(
            vector_totals[6].astype(jnp.bfloat16), "dp", scatter_dimension=0, tiled=True
        ).astype(jnp.float32),
        lax.psum_scatter(
            vector_totals[7].astype(jnp.bfloat16), "dp", scatter_dimension=0, tiled=True
        ).astype(jnp.float32),
    )
    block_stack = jnp.stack(block_outs, axis=0)[:, None]
    grad_stack = jnp.stack(input_grads, axis=0)[:, None]
    return (
        block_stack,
        grad_stack,
        summed[4],
        summed[5],
        summed[0],
        summed[6],
        summed[1],
        summed[7],
        summed[8],
        summed[9],
        summed[2],
        summed[10],
        summed[3],
        summed[11],
    )


def solution(mesh):
    placed = (
        P(None, "dp", "ctx", None),
        P(None, "dp", None),
        P("dp"),
        P("dp"),
        P("ctx", "dp"),
        P("dp"),
        P("ctx", "dp"),
        P("dp"),
        P("dp"),
        P("dp"),
        P("ctx", "dp"),
        P("dp"),
        P("ctx", "dp"),
        P("dp"),
        P(None, "dp", "ctx", None),
    )
    return jax.shard_map(
        local,
        mesh=mesh,
        in_specs=placed,
        out_specs=(
            P(None, "dp", "ctx", None),
            P(None, "dp", "ctx", None),
            P("dp"),
            P("dp"),
            P("ctx", "dp"),
            P("dp"),
            P("ctx", "dp"),
            P("dp"),
            P("dp"),
            P("dp"),
            P("ctx", "dp"),
            P("dp"),
            P("ctx", "dp"),
            P("dp"),
        ),
        check_vma=False,
    )
```

profile of v0, /device:TPU:0, one launch (start us, length us, event | category | flops | bytes accessed | tf_op | source)
XLA Modules:
  0.0 1375.5 jit_solution(13791595088519105775)
XLA Ops:
  8.7 18.1 %all-gather = bf16[4,816,136]{1,2,0:T(8,128)(2,1)S(1)} all-gather(bf16[1,816,136]{1,2,0:T(8,128)(2,1)} %bitcast.544), channel_id=1, replica_groups=mesh['dp'=4,'ctx'=8] {'dp'}, dimensions={0}, use_global_device_ids=true | all-gather | bytes 1109760 | tf_op jit(solution)/shard_map/all_gather | solution.py:95
  52.4 16.3 %all-reduce.20 = (bf16[2176]{0:T(1024)(128)(2,1)S(1)}, bf16[1088]{0:T(1024)(128)(2,1)S(1)}, bf16[1088]{0:T(1024)(128)(2,1)S(1)}, bf16[1088]{0:T(1024)(128)(2,1)S...) all-reduce(bf16[2176]{0:T(1024)(128)(2,1)S(1)} %dynamic-update-slic, ...), channel_id=1, replica_groups=mesh['dp'=4,'ctx'=8] {'dp'}, use_global_device_ids=true, to_apply=%add.2 | all-reduce | flops 11968 | bytes 47872
  78.6 71.2 %all-gather.10.cloned.1.call-done = bf16[1088,3264]{1,0:T(8,128)(2,1)} async-done(((bf16[136,3264]{1,0:T(8,128)(2,1)}), bf16[1088,3264]{1,0:T(8,128)(2,1)}) %all-gather.10.cloned.1.call-update) | async-done | bytes 7102480 | tf_op jit(solution)/shard_map/all_gather | solution.py:109
  161.3 90.9 %while.116 = (s32[]{:T(128)}, bf16[64,2176]{1,0:T(8,128)(2,1)S(1)}, f32[17,64]{1,0:T(8,128)S(1)}, f32[17,64]{1,0:T(8,128)S(1)}, f32[17,64,64]{2,1,0:T(8,128)S(1)...) while((s32[]{:T(128)}, bf16[64,2176]{1,0:T(8,128)(2,1)S(1)}, ...), condition=%wide.region_36.37_spmd.clone, body=%wide.region_32.0_spmd.clone.sunk | while | flops 18471876 | bytes 4675807 | solution.py:176
  215.5 14.6 %collective-permute-start.2 = (bf16[64,2176]{1,0:T(8,128)(2,1)S(1)}, bf16[64,2176]{1,0:T(8,128)(2,1)S(1)}, u32[]{:S(2)}, u32[]{:S(2)}) collective-permute-start(bf16[64,2176]{1,0:T(8,128)(2,1)S(1)} %get-tuple-element.2502), channel_id=1, source_target_pairs={{0,1},{1,2},{2,3},{3,4},{4,5},{5,6},{6,7},{8,9},{9,10},{10,11},{11... | collective-permute-start | bytes 835592 | tf_op jit(solution)/shard_map/while/body/eval_jaxpr/ppermute | solution.py:18
  232.8 16.7 %collective-permute-start.2 = (bf16[64,2176]{1,0:T(8,128)(2,1)S(1)}, bf16[64,2176]{1,0:T(8,128)(2,1)S(1)}, u32[]{:S(2)}, u32[]{:S(2)}) collective-permute-start(bf16[64,2176]{1,0:T(8,128)(2,1)S(1)} %get-tuple-element.2502), channel_id=1, source_target_pairs={{0,1},{1,2},{2,3},{3,4},{4,5},{5,6},{6,7},{8,9},{9,10},{10,11},{11... | collective-permute-start | bytes 835592 | tf_op jit(solution)/shard_map/while/body/eval_jaxpr/ppermute | solution.py:18
  255.4 132.9 %while.115 = (s32[]{:T(128)}, bf16[64,2176]{1,0:T(8,128)(2,1)S(1)}, f32[17,64]{1,0:T(8,128)S(1)}, f32[17,64]{1,0:T(8,128)S(1)}, f32[17,64,64]{2,1,0:T(8,128)S(1)...) while((s32[]{:T(128)}, bf16[64,2176]{1,0:T(8,128)(2,1)S(1)}, ...), condition=%wide.region_23.24_spmd.clone, body=%wide.region_19.0_spmd.clone.sunk | while | flops 18471876 | bytes 4675807 | solution.py:176
  255.4 19.0 %collective-permute-start.1 = (bf16[64,2176]{1,0:T(8,128)(2,1)S(1)}, bf16[64,2176]{1,0:T(8,128)(2,1)S(1)}, u32[]{:S(2)}, u32[]{:S(2)}) collective-permute-start(bf16[64,2176]{1,0:T(8,128)(2,1)S(1)} %get-tuple-element.2541), channel_id=1, source_target_pairs={{0,1},{1,2},{2,3},{3,4},{4,5},{5,6},{6,7},{8,9},{9,10},{10,11},{11... | collective-permute-start | bytes 835592 | tf_op jit(solution)/shard_map/while/body/eval_jaxpr/ppermute | solution.py:18
  277.0 13.9 %collective-permute-start.1 = (bf16[64,2176]{1,0:T(8,128)(2,1)S(1)}, bf16[64,2176]{1,0:T(8,128)(2,1)S(1)}, u32[]{:S(2)}, u32[]{:S(2)}) collective-permute-start(bf16[64,2176]{1,0:T(8,128)(2,1)S(1)} %get-tuple-element.2541), channel_id=1, source_target_pairs={{0,1},{1,2},{2,3},{3,4},{4,5},{5,6},{6,7},{8,9},{9,10},{10,11},{11... | collective-permute-start | bytes 835592 | tf_op jit(solution)/shard_map/while/body/eval_jaxpr/ppermute | solution.py:18
  293.5 18.1 %collective-permute-start.1 = (bf16[64,2176]{1,0:T(8,128)(2,1)S(1)}, bf16[64,2176]{1,0:T(8,128)(2,1)S(1)}, u32[]{:S(2)}, u32[]{:S(2)}) collective-permute-start(bf16[64,2176]{1,0:T(8,128)(2,1)S(1)} %get-tuple-element.2541), channel_id=1, source_target_pairs={{0,1},{1,2},{2,3},{3,4},{4,5},{5,6},{6,7},{8,9},{9,10},{10,11},{11... | collective-permute-start | bytes 835592 | tf_op jit(solution)/shard_map/while/body/eval_jaxpr/ppermute | solution.py:18
  344.8 18.5 %collective-permute-start.1 = (bf16[64,2176]{1,0:T(8,128)(2,1)S(1)}, bf16[64,2176]{1,0:T(8,128)(2,1)S(1)}, u32[]{:S(2)}, u32[]{:S(2)}) collective-permute-start(bf16[64,2176]{1,0:T(8,128)(2,1)S(1)} %get-tuple-element.2541), channel_id=1, source_target_pairs={{0,1},{1,2},{2,3},{3,4},{4,5},{5,6},{6,7},{8,9},{9,10},{10,11},{11... | collective-permute-start | bytes 835592 | tf_op jit(solution)/shard_map/while/body/eval_jaxpr/ppermute | solution.py:18
  365.9 19.7 %collective-permute-start.1 = (bf16[64,2176]{1,0:T(8,128)(2,1)S(1)}, bf16[64,2176]{1,0:T(8,128)(2,1)S(1)}, u32[]{:S(2)}, u32[]{:S(2)}) collective-permute-start(bf16[64,2176]{1,0:T(8,128)(2,1)S(1)} %get-tuple-element.2541), channel_id=1, source_target_pairs={{0,1},{1,2},{2,3},{3,4},{4,5},{5,6},{6,7},{8,9},{9,10},{10,11},{11... | collective-permute-start | bytes 835592 | tf_op jit(solution)/shard_map/while/body/eval_jaxpr/ppermute | solution.py:18
  391.9 72.6 %while.114 = (s32[]{:T(128)}, bf16[64,2176]{1,0:T(8,128)(2,1)S(1)}, f32[17,64]{1,0:T(8,128)S(1)}, f32[17,64]{1,0:T(8,128)S(1)}, f32[17,64,64]{2,1,0:T(8,128)S(1)...) while((s32[]{:T(128)}, bf16[64,2176]{1,0:T(8,128)(2,1)S(1)}, ...), condition=%wide.region_10.11_spmd.clone, body=%wide.region_6.0_spmd.clone.sunk | while | flops 18471876 | bytes 4675807 | solution.py:176
  525.6 116.1 %while.118 = (s32[]{:T(128)}, bf16[64,2176]{1,0:T(8,128)(2,1)S(1)}, f32[64,2176]{1,0:T(8,128)}, f32[17,64,64]{2,1,0:T(8,128)}, s32[]{:T(128)}, /*index=5*/s32[4]...) while((s32[]{:T(128)}, bf16[64,2176]{1,0:T(8,128)(2,1)S(1)}, ...), condition=%wide.region_52.53_spmd.clone, body=%wide.region_50.52_spmd.clone.sunk | while | flops 46043972 | bytes 20630664 | solution.py:296
  651.5 109.3 %while.117 = (s32[]{:T(128)}, bf16[64,2176]{1,0:T(8,128)(2,1)S(1)}, f32[64,2176]{1,0:T(8,128)}, f32[17,64,64]{2,1,0:T(8,128)}, s32[]{:T(128)}, /*index=5*/s32[4]...) while((s32[]{:T(128)}, bf16[64,2176]{1,0:T(8,128)(2,1)S(1)}, ...), condition=%wide.region_44.45_spmd.clone, body=%wide.region_42.44_spmd.clone.sunk | while | flops 46043972 | bytes 20630564 | solution.py:296
  774.4 118.4 %while.119 = (s32[]{:T(128)}, bf16[64,2176]{1,0:T(8,128)(2,1)S(1)}, f32[64,2176]{1,0:T(8,128)}, f32[17,64,64]{2,1,0:T(8,128)}, s32[]{:T(128)}, /*index=5*/s32[4]...) while((s32[]{:T(128)}, bf16[64,2176]{1,0:T(8,128)(2,1)S(1)}, ...), condition=%wide.region_60.61_spmd.clone, body=%wide.region_58.60_spmd.clone.sunk | while | flops 46043972 | bytes 19516388 | solution.py:296
  960.8 15.9 %convolution_add_fusion.4 = f32[1088,4352]{1,0:T(8,128)} fusion(f32[1088,4352]{1,0:T(8,128)} %fusion.222, bf16[64,4352]{1,0:T(8,128)(2,1)S(1)} %copy-done.104, f32[64,1088]{1,0:T(8,128)S(1)} %copy-done.33, f32[64]{0:T(128)S(1)} %copy-done.155, f32[64]{0:T(128)S(1)} %copy-done.141, f32[1088]{0:T(1024)S(1)} %copy-done.111, f32[1088]{0:T(1024)S(1)} %convert_element_type.477), kind=kOutput, calls=%fused_computation.103 | convolution fusion | flops 611160064 | bytes 38724608 | tf_op jit(solution)/shard_map/dot_general | solution.py:46
  1012.8 16.8 %all-reduce.19 = (bf16[1088]{0:T(1024)(128)(2,1)S(1)}, bf16[1088]{0:T(1024)(128)(2,1)S(1)}, bf16[1088]{0:T(1024)(128)(2,1)S(1)}, bf16[2176]{0:T(1024)(128)(2,1)S...) all-reduce(bf16[1088]{0:T(1024)(128)(2,1)S(1)} %copy-done.157, ...), channel_id=1, replica_groups=mesh['dp'=4,'ctx'=8] {'dp'}, use_global_device_ids=true, to_apply=%add.7 | all-reduce | flops 14144 | bytes 56576
  1030.7 74.7 %reduce-scatter.21.cloned.1.call-done = bf16[544,1088]{1,0:T(8,128)(2,1)} async-done(((bf16[4352,1088]{1,0:T(8,128)(2,1)}), bf16[544,1088]{1,0:T(8,128)(2,1)}) %reduce-scatter.21.cloned.1.call-update) | async-done | bytes 1183760 | tf_op jit(solution)/shard_map/reduce_scatter | solution.py:385
  1117.7 88.4 %reduce-scatter.19.cloned.1.call-done = bf16[136,4352]{1,0:T(8,128)(2,1)} async-done(((bf16[1088,4352]{1,0:T(8,128)(2,1)}), bf16[136,4352]{1,0:T(8,128)(2,1)}) %reduce-scatter.19.cloned.1.call-update) | async-done | bytes 1183760 | tf_op jit(solution)/shard_map/reduce_scatter | solution.py:382
  1211.1 26.1 %all-reduce.18 = (bf16[272]{0:T(512)(128)(2,1)S(1)}, bf16[272]{0:T(512)(128)(2,1)S(1)}, bf16[544]{0:T(1024)(128)(2,1)S(1)}, bf16[272]{0:T(512)(128)(2,1)S(1)}, b...) all-reduce(bf16[272]{0:T(512)(128)(2,1)S(1)} %dynamic-slice.9, ...), channel_id=1, replica_groups=mesh['dp'=4,'ctx'=8] {'ctx'}, use_global_device_ids=true, to_apply=%region_66.67 | all-reduce | flops 3264 | bytes 13056 | tf_op jit(solution)/shard_map/psum | solution.py:390
  1252.2 15.6 %reduce-scatter.23.cloned.1.call-done = bf16[816,136]{1,0:T(8,128)(2,1)} async-done(((bf16[3264,136]{1,0:T(8,128)(2,1)}), bf16[816,136]{1,0:T(8,128)(2,1)}) %reduce-scatter.23.cloned.1.call-update) | async-done | bytes 221968
  1269.8 57.3 %all-reduce.23.cloned.1.call-done = bf16[544,1088]{1,0:T(8,128)(2,1)} async-done(((bf16[544,1088]{1,0:T(8,128)(2,1)}), bf16[544,1088]{1,0:T(8,128)(2,1)}) %all-reduce.23.cloned.1.call-update) | async-done | bytes 1183760
  1329.5 37.0 %reduce-scatter.27.cloned.1.call-done = bf16[1088,136]{1,0:T(8,128)(2,1)} async-done(((bf16[4352,136]{1,0:T(8,128)(2,1)}), bf16[1088,136]{1,0:T(8,128)(2,1)}) %reduce-scatter.27.cloned.1.call-update) | async-done | bytes 295952
  (1884 shorter events, 789.6 us)
Async XLA Ops:
  7.2 36.4 %all-gather.20.cloned.1.call-start = ((), (), s32[]{:S(2)}) async-start(), calls=%async_computation.15 | async-start | bytes 1566720 | tf_op jit(solution)/shard_map/all_gather | solution.py:97
  7.9 67.7 %all-gather.16.cloned.1.call-start = ((), (), s32[]{:S(2)}) async-start(), calls=%async_computation.10 | async-start | bytes 1740800 | tf_op jit(solution)/shard_map/all_gather | solution.py:98
  8.7 141.1 %all-gather.10.cloned.1.call-start = ((), (), s32[]{:S(2)}) async-start(), calls=%async_computation.7 | async-start | bytes 8146944 | tf_op jit(solution)/shard_map/all_gather | solution.py:109
  28.9 438.3 %all-gather.12.cloned.1.call-start = ((), (), s32[]{:S(2)}) async-start(), calls=%async_computation.8 | async-start | bytes 2820096 | tf_op jit(solution)/shard_map/all_gather | solution.py:110
  41.2 433.4 %all-gather.14.cloned.1.call-start = ((), (), s32[]{:S(2)}) async-start(), calls=%async_computation.9 | async-start | bytes 10653696 | tf_op jit(solution)/shard_map/all_gather | solution.py:111
  47.4 433.5 %all-gather.18.cloned.1.call-start = ((), (), s32[]{:S(2)}) async-start(), calls=%async_computation.11 | async-start | bytes 11280384 | tf_op jit(solution)/shard_map/all_gather | solution.py:112
  78.2 928.7 %reduce-scatter.29.cloned.1.call-start = ((), (), s32[]{:S(2)}) async-start(), calls=%async_computation.20 | async-start | bytes 2820096
  215.5 15.8 %collective-permute-start.2 = (bf16[64,2176]{1,0:T(8,128)(2,1)S(1)}, bf16[64,2176]{1,0:T(8,128)(2,1)S(1)}, u32[]{:S(2)}, u32[]{:S(2)}) collective-permute-start(bf16[64,2176]{1,0:T(8,128)(2,1)S(1)} %get-tuple-element.2502), channel_id=1, source_target_pairs={{0,1},{1,2},{2,3},{3,4},{4,5},{5,6},{6,7},{8,9},{9,10},{10,11},{11... | collective-permute-start | bytes 835592 | tf_op jit(solution)/shard_map/while/body/eval_jaxpr/ppermute | solution.py:18
  232.8 17.9 %collective-permute-start.2 = (bf16[64,2176]{1,0:T(8,128)(2,1)S(1)}, bf16[64,2176]{1,0:T(8,128)(2,1)S(1)}, u32[]{:S(2)}, u32[]{:S(2)}) collective-permute-start(bf16[64,2176]{1,0:T(8,128)(2,1)S(1)} %get-tuple-element.2502), channel_id=1, source_target_pairs={{0,1},{1,2},{2,3},{3,4},{4,5},{5,6},{6,7},{8,9},{9,10},{10,11},{11... | collective-permute-start | bytes 835592 | tf_op jit(solution)/shard_map/while/body/eval_jaxpr/ppermute | solution.py:18
  255.4 20.1 %collective-permute-start.1 = (bf16[64,2176]{1,0:T(8,128)(2,1)S(1)}, bf16[64,2176]{1,0:T(8,128)(2,1)S(1)}, u32[]{:S(2)}, u32[]{:S(2)}) collective-permute-start(bf16[64,2176]{1,0:T(8,128)(2,1)S(1)} %get-tuple-element.2541), channel_id=1, source_target_pairs={{0,1},{1,2},{2,3},{3,4},{4,5},{5,6},{6,7},{8,9},{9,10},{10,11},{11... | collective-permute-start | bytes 835592 | tf_op jit(solution)/shard_map/while/body/eval_jaxpr/ppermute | solution.py:18
  277.0 15.0 %collective-permute-start.1 = (bf16[64,2176]{1,0:T(8,128)(2,1)S(1)}, bf16[64,2176]{1,0:T(8,128)(2,1)S(1)}, u32[]{:S(2)}, u32[]{:S(2)}) collective-permute-start(bf16[64,2176]{1,0:T(8,128)(2,1)S(1)} %get-tuple-element.2541), channel_id=1, source_target_pairs={{0,1},{1,2},{2,3},{3,4},{4,5},{5,6},{6,7},{8,9},{9,10},{10,11},{11... | collective-permute-start | bytes 835592 | tf_op jit(solution)/shard_map/while/body/eval_jaxpr/ppermute | solution.py:18
  293.5 19.2 %collective-permute-start.1 = (bf16[64,2176]{1,0:T(8,128)(2,1)S(1)}, bf16[64,2176]{1,0:T(8,128)(2,1)S(1)}, u32[]{:S(2)}, u32[]{:S(2)}) collective-permute-start(bf16[64,2176]{1,0:T(8,128)(2,1)S(1)} %get-tuple-element.2541), channel_id=1, source_target_pairs={{0,1},{1,2},{2,3},{3,4},{4,5},{5,6},{6,7},{8,9},{9,10},{10,11},{11... | collective-permute-start | bytes 835592 | tf_op jit(solution)/shard_map/while/body/eval_jaxpr/ppermute | solution.py:18
  344.8 19.6 %collective-permute-start.1 = (bf16[64,2176]{1,0:T(8,128)(2,1)S(1)}, bf16[64,2176]{1,0:T(8,128)(2,1)S(1)}, u32[]{:S(2)}, u32[]{:S(2)}) collective-permute-start(bf16[64,2176]{1,0:T(8,128)(2,1)S(1)} %get-tuple-element.2541), channel_id=1, source_target_pairs={{0,1},{1,2},{2,3},{3,4},{4,5},{5,6},{6,7},{8,9},{9,10},{10,11},{11... | collective-permute-start | bytes 835592 | tf_op jit(solution)/shard_map/while/body/eval_jaxpr/ppermute | solution.py:18
  365.9 20.9 %collective-permute-start.1 = (bf16[64,2176]{1,0:T(8,128)(2,1)S(1)}, bf16[64,2176]{1,0:T(8,128)(2,1)S(1)}, u32[]{:S(2)}, u32[]{:S(2)}) collective-permute-start(bf16[64,2176]{1,0:T(8,128)(2,1)S(1)} %get-tuple-element.2541), channel_id=1, source_target_pairs={{0,1},{1,2},{2,3},{3,4},{4,5},{5,6},{6,7},{8,9},{9,10},{10,11},{11... | collective-permute-start | bytes 835592 | tf_op jit(solution)/shard_map/while/body/eval_jaxpr/ppermute | solution.py:18
  391.9 14.1 %collective-permute-start = (bf16[64,2176]{1,0:T(8,128)(2,1)S(1)}, bf16[64,2176]{1,0:T(8,128)(2,1)S(1)}, u32[]{:S(2)}, u32[]{:S(2)}) collective-permute-start(bf16[64,2176]{1,0:T(8,128)(2,1)S(1)} %get-tuple-element.2580), channel_id=1, source_target_pairs={{0,1},{1,2},{2,3},{3,4},{4,5},{5,6},{6,7},{8,9},{9,10},{10,11},{11... | collective-permute-start | bytes 835592 | tf_op jit(solution)/shard_map/while/body/eval_jaxpr/ppermute | solution.py:18
  773.5 235.8 %reduce-scatter.17.cloned.1.call-start = ((), (), s32[]{:S(2)}) async-start(), calls=%async_computation.12 | async-start | bytes 8146944 | tf_op jit(solution)/shard_map/reduce_scatter | solution.py:376
  790.5 15.2 %collective-permute-start.8 = (bf16[64,2176]{1,0:T(8,128)(2,1)S(1)}, bf16[64,2176]{1,0:T(8,128)(2,1)S(1)}, u32[]{:S(2)}, u32[]{:S(2)}) collective-permute-start(bf16[64,2176]{1,0:T(8,128)(2,1)S(1)} %copy.552), channel_id=1, source_target_pairs={{0,1},{1,2},{2,3},{3,4},{4,5},{5,6},{6,7},{7,0},{8,9},{9,10},{10,1... | collective-permute-start | bytes 835592 | tf_op jit(solution)/shard_map/while/body/eval_jaxpr/ppermute | solution.py:24
  810.2 19.0 %collective-permute-start.8 = (bf16[64,2176]{1,0:T(8,128)(2,1)S(1)}, bf16[64,2176]{1,0:T(8,128)(2,1)S(1)}, u32[]{:S(2)}, u32[]{:S(2)}) collective-permute-start(bf16[64,2176]{1,0:T(8,128)(2,1)S(1)} %copy.552), channel_id=1, source_target_pairs={{0,1},{1,2},{2,3},{3,4},{4,5},{5,6},{6,7},{7,0},{8,9},{9,10},{10,1... | collective-permute-start | bytes 835592 | tf_op jit(solution)/shard_map/while/body/eval_jaxpr/ppermute | solution.py:24
  915.2 190.3 %reduce-scatter.21.cloned.1.call-start = ((), (), s32[]{:S(2)}) async-start(), calls=%async_computation.14 | async-start | bytes 11280384 | tf_op jit(solution)/shard_map/reduce_scatter | solution.py:385
  950.4 255.7 %reduce-scatter.19.cloned.1.call-start = ((), (), s32[]{:S(2)}) async-start(), calls=%async_computation.13 | async-start | bytes 10653696 | tf_op jit(solution)/shard_map/reduce_scatter | solution.py:382
  989.6 260.8 %reduce-scatter.25.cloned.1.call-start = ((), (), s32[]{:S(2)}) async-start(), calls=%async_computation.17 | async-start | bytes 696320
  1009.1 258.7 %reduce-scatter.23.cloned.1.call-start = ((), (), s32[]{:S(2)}) async-start(), calls=%async_computation.16 | async-start | bytes 2088960
  1012.1 315.0 %all-reduce.23.cloned.1.call-start = ((), (), s32[]{:S(2)}) async-start(), calls=%async_computation.19 | async-start | bytes 2506752
  1105.5 261.0 %reduce-scatter.27.cloned.1.call-start = ((), (), s32[]{:S(2)}) async-start(), calls=%async_computation.18 | async-start | bytes 2785280
  (440 other events, 3677.0 us)
Sparse Core Ops, SparseCore 0:
  9.9 33.6 all-gather.19
  45.4 30.1 all-gather.15
  77.3 72.4 all-gather.9
  151.8 31.2 all-gather.11
  184.6 100.2 all-gather.13
  286.4 110.0 all-gather.17
  773.6 49.7 reduce-scatter.28
  915.3 84.3 reduce-scatter.16
  1002.0 103.4 reduce-scatter.20
  1107.6 98.4 reduce-scatter.18
  1209.6 23.2 reduce-scatter.24
  1236.1 31.6 reduce-scatter.22
  1271.3 55.7 all-reduce.22
  1330.0 36.5 reduce-scatter.26
where the time goes:
time: 1390 us; the launch traced here: 1380 us
  starting transfers between devices  423 us (30%)
  waiting for transfers between devices  377 us (27%)
  matrix products  265 us (19%)
  local copies, waits for them, and re-layouts  129 us (9%)
  blocking collectives  88.5 us (6%)
  other arithmetic  64.8 us (5%)
  between operations  20.5 us (1%)
    ppermute x45, starting transfers between devices, passed_along(): return lax.ppermute(block, axis, route)  343 us
    unnamed x19, waiting for transfers between devices  112 us
    dot_general x12, matrix products, outer_sum(): lax.dot_general(left, right, (((0,), (0,)), ((), ())), preferred_element_...  100 us
    reduce_scatter x1, waiting for transfers between devices, local(): lax.psum_scatter(totals[2].astype(jnp.bfloat16), 'ctx', scatter_dimension...  88.4 us
    ppermute x24, starting transfers between devices, from_behind(): return lax.ppermute(value, axis, pairs)  78.7 us
    reduce_scatter x1, waiting for transfers between devices, local(): lax.psum_scatter(totals[3].astype(jnp.bfloat16), 'ctx', scatter_dimension...  74.7 us
    all_gather x1, waiting for transfers between devices, gather_all(): lax.all_gather(rows_full[0], 'ctx', axis=0, tiled=True)  71.2 us
    dot_general x12, matrix products, back_dot(): lax.dot_general(gradient, weight, (((1,), (1,)), ((), ())), preferred_ele...  49.7 us
  transfers between devices with their start and end apart: 83, of which 30 were waited for; matrix products, arithmetic and copies ran while one was open for 22% of the time, Pallas kernels for 0%

commit v1 on v0

v1 whole, which is shorter than its diff:
```python
import jax
import jax.numpy as jnp
from jax import lax
from jax.sharding import PartitionSpec as P

HEADS = 17
HEAD_DIM = 64


EPSILON = 1e-05
SCALE = 0.125
NEGATIVE = -1e30


def layer_norm(values, scale, shift):
    row_mean = jnp.mean(values, axis=-1, keepdims=True)
    centered = values - row_mean
    variance = jnp.mean(centered * centered, axis=-1, keepdims=True)
    inverse = lax.rsqrt(variance + EPSILON)
    normal = centered * inverse
    return (normal * scale + shift, normal, inverse)


def norm_back(grad_normed, normal, inverse, scale):
    scaled = grad_normed * scale
    return inverse * (
        scaled
        - jnp.mean(scaled, axis=-1, keepdims=True)
        - normal * jnp.mean(scaled * normal, axis=-1, keepdims=True)
    )


def outer_sum(left, right):
    return lax.dot_general(
        left, right, (((0,), (0,)), ((), ())), preferred_element_type=jnp.float32
    )


def back_dot(gradient, weight):
    return lax.dot_general(
        gradient, weight, (((1,), (1,)), ((), ())), preferred_element_type=jnp.float32
    )


def doc_numbers(positions, seq_ends):
    return jnp.sum((positions[None, :, None] >= seq_ends[:, None, :]).astype(jnp.int32), axis=2)


def heads_first(rows):
    devices, micro, span, columns = rows.shape
    parts = rows.reshape(devices, micro, span, columns // HEAD_DIM, HEAD_DIM)
    parts = jnp.transpose(parts, (1, 3, 0, 2, 4))
    return parts.reshape(micro, columns // HEAD_DIM, devices * span, HEAD_DIM)


def rows_first(per_head, devices):
    micro, heads, stream, _ = per_head.shape
    parts = per_head.reshape(micro, heads, devices, stream // devices, HEAD_DIM)
    parts = jnp.transpose(parts, (2, 0, 3, 1, 4))
    return parts.reshape(devices, micro, stream // devices, heads * HEAD_DIM)


def batched(left, right, left_dim, right_dim):
    return lax.dot_general(
        left,
        right,
        (((left_dim,), (right_dim,)), ((0, 1), (0, 1))),
        preferred_element_type=jnp.float32,
    )


def dot32(left, right):
    return jnp.dot(left, right, preferred_element_type=jnp.float32)


def piece_route(dp_size, ctx_size):
    return [
        (q * ctx_size + r, r * dp_size + q) for q in range(dp_size) for r in range(ctx_size)
    ]


def local(
    inputs,
    lengths,
    ln1_scale,
    ln1_bias,
    w_qkv,
    qv_bias,
    w_out,
    out_bias,
    ln2_scale,
    ln2_bias,
    w_up,
    up_bias,
    w_down,
    down_bias,
    out_grad,
):
    ctx_index = lax.axis_index("ctx")
    ctx_size = lax.axis_size("ctx")
    dp_size = lax.axis_size("dp")
    micro, _, span, width = inputs.shape
    rows = micro * span
    stream = span * ctx_size
    qkv_part = w_qkv.shape[1]
    out_part = w_out.shape[1]
    bf16 = jnp.bfloat16
    f32 = jnp.float32

    tokens32 = inputs.reshape(rows, width).astype(f32)
    grad_out = out_grad.reshape(rows, width)
    grad32 = grad_out.astype(f32)

    small = (ln1_scale, ln1_bias, qv_bias, out_bias, ln2_scale, ln2_bias, down_bias)
    small_all = lax.all_gather(jnp.concatenate(small), "dp", axis=0)
    vectors = []
    start = 0
    for member in small:
        size = member.shape[0]
        vectors.append(small_all[:, start : start + size].reshape(-1).astype(f32))
        start += size
    ln1_scale, ln1_bias, qv_bias, out_bias, ln2_scale, ln2_bias, down_bias = vectors
    qkv_all = lax.all_gather(lax.all_gather(w_qkv, "ctx", axis=0, tiled=True), "dp", axis=0)
    out_all = lax.all_gather(lax.all_gather(w_out, "ctx", axis=0, tiled=True), "dp", axis=0)
    out_full = jnp.concatenate([out_all[j] for j in range(dp_size)], axis=1)
    up_here = lax.all_gather(w_up, "ctx", axis=0, tiled=True)
    down_piece = lax.all_to_all(w_down, "dp", split_axis=0, concat_axis=1, tiled=True)
    route = piece_route(dp_size, ctx_size)
    down_piece = lax.ppermute(down_piece, ("dp", "ctx"), route)
    down_here = lax.all_gather(down_piece, "ctx", axis=0, tiled=True)
    grad_all = lax.all_gather(grad_out, "dp", axis=0, tiled=True)

    normed1, normal1, inverse1 = layer_norm(tokens32, ln1_scale, ln1_bias)
    normed1 = normed1.astype(bf16)
    qkv_bias = jnp.concatenate([qv_bias[:width], jnp.zeros((width,), f32), qv_bias[width:]])
    qkv = jnp.concatenate([dot32(normed1, qkv_all[j]) for j in range(dp_size)], axis=1)
    qkv = (qkv + qkv_bias).astype(bf16)
    kv_all = lax.all_gather(qkv[:, width:].reshape(micro, span, 2 * width), "ctx", axis=0)
    kv_heads = heads_first(kv_all)
    keys, values = kv_heads[:, :HEADS], kv_heads[:, HEADS:]
    queries = heads_first(qkv[:, :width].reshape(1, micro, span, width))
    seq_ends = jnp.cumsum(lengths[:, 0], axis=1)
    key_pos = jnp.arange(stream, dtype=jnp.int32)
    query_pos = ctx_index * span + jnp.arange(span, dtype=jnp.int32)
    key_doc = doc_numbers(key_pos, seq_ends)
    query_doc = doc_numbers(query_pos, seq_ends)
    visible = (key_doc[:, None, :] == query_doc[:, :, None]) & (
        key_pos[None, None, :] <= query_pos[None, :, None]
    )
    scores = batched(queries, keys, 3, 3) * SCALE
    scores = jnp.where(visible[:, None], scores, NEGATIVE)
    weights = jnp.exp(scores - jnp.max(scores, axis=-1, keepdims=True))
    weights = (weights / jnp.sum(weights, axis=-1, keepdims=True)).astype(bf16)
    attended_heads = batched(weights, values, 3, 2)
    attended = rows_first(attended_heads.astype(bf16), 1).reshape(rows, width)
    residual = tokens32 + dot32(attended, out_full) + out_bias
    normed2, normal2, inverse2 = layer_norm(residual, ln2_scale, ln2_bias)
    normed2_all = lax.all_gather(normed2.astype(bf16), "dp", axis=0, tiled=True)

    gelu_input = dot32(normed2_all, up_here) + up_bias.astype(f32)
    hidden, gelu_pull = jax.vjp(jax.nn.gelu, gelu_input)
    hidden = hidden.astype(bf16)
    grad_upper = gelu_pull(back_dot(grad_all, down_here))[0].astype(bf16)
    both = jnp.concatenate(
        [dot32(hidden, down_here).astype(bf16), back_dot(grad_upper, up_here).astype(bf16)], axis=1
    )
    both = lax.psum_scatter(
        both.reshape(dp_size, rows, 2 * width), "dp", scatter_dimension=0
    ).astype(f32)
    block_out = (residual + both[:, :width] + down_bias).astype(bf16)
    grad_normed2 = both[:, width:]
    up_grad = lax.psum_scatter(
        outer_sum(normed2_all, grad_upper).astype(bf16), "ctx", scatter_dimension=0, tiled=True
    ).astype(f32)
    down_grad = lax.psum_scatter(
        outer_sum(hidden, grad_all).astype(bf16), "ctx", scatter_dimension=0, tiled=True
    )
    down_grad = lax.ppermute(down_grad, ("dp", "ctx"), [(b, a) for a, b in route])
    down_grad = lax.all_to_all(
        down_grad, "dp", split_axis=1, concat_axis=0, tiled=True
    ).astype(f32)

    grad_residual = grad32 + norm_back(grad_normed2, normal2, inverse2, ln2_scale)
    grad_branch = grad_residual.astype(bf16)
    grad_attended = back_dot(grad_branch, out_full).astype(bf16)
    out_grads = jnp.stack(
        [
            outer_sum(attended, grad_branch[:, j * out_part : (j + 1) * out_part])
            for j in range(dp_size)
        ]
    ).astype(bf16)
    out_grads = lax.psum_scatter(out_grads, "dp", scatter_dimension=0)
    out_grads = out_grads.reshape(ctx_size, -1, out_part)
    out_grads = lax.psum_scatter(out_grads, "ctx", scatter_dimension=0).astype(f32)
    grad_heads = heads_first(grad_attended.reshape(1, micro, span, width))
    row_dot = jnp.sum(grad_heads.astype(f32) * attended_heads, axis=-1, keepdims=True)
    grad_weights = batched(grad_heads, values, 3, 3)
    grad_scores = (weights.astype(f32) * (grad_weights - row_dot)).astype(bf16)
    grad_queries = batched(grad_scores, keys, 3, 2) * SCALE
    grad_keys = batched(grad_scores, queries, 2, 2) * SCALE
    grad_values = batched(weights, grad_heads, 2, 2)
    grad_kv = rows_first(
        jnp.concatenate([grad_keys.astype(bf16), grad_values.astype(bf16)], axis=1), ctx_size
    )
    grad_kv = lax.psum_scatter(grad_kv, "ctx", scatter_dimension=0).reshape(rows, 2 * width)
    grad_qkv = jnp.concatenate(
        [rows_first(grad_queries.astype(bf16), 1).reshape(rows, width), grad_kv], axis=1
    )
    pieces = [grad_qkv[:, j * qkv_part : (j + 1) * qkv_part] for j in range(dp_size)]
    qkv_grads = jnp.stack([outer_sum(normed1, piece) for piece in pieces]).astype(bf16)
    qkv_grads = lax.psum_scatter(qkv_grads, "dp", scatter_dimension=0)
    qkv_grads = qkv_grads.reshape(ctx_size, -1, qkv_part)
    qkv_grads = lax.psum_scatter(qkv_grads, "ctx", scatter_dimension=0).astype(f32)
    grad_normed1 = back_dot(pieces[0], qkv_all[0])
    for j in range(1, dp_size):
        grad_normed1 = grad_normed1 + back_dot(pieces[j], qkv_all[j])
    input_grad = (grad_residual + norm_back(grad_normed1, normal1, inverse1, ln1_scale)).astype(
        bf16
    )

    qkv_sums = jnp.sum(grad_qkv.astype(f32), axis=0)
    sums = (
        jnp.sum(grad_normed1 * normal1, axis=0),
        jnp.sum(grad_normed1, axis=0),
        jnp.concatenate([qkv_sums[:width], qkv_sums[2 * width :]]),
        jnp.sum(grad_branch.astype(f32), axis=0),
        jnp.sum(grad_normed2 * normal2, axis=0),
        jnp.sum(grad_normed2, axis=0),
        jnp.sum(grad32, axis=0),
    )
    sums = jnp.concatenate([member.reshape(dp_size, -1) for member in sums], axis=1)
    sums = lax.psum_scatter(sums, "dp", scatter_dimension=0)
    up_sums = jnp.sum(grad_upper.astype(f32), axis=0)
    sums = lax.psum(jnp.concatenate([sums, up_sums]), "ctx")
    cuts = []
    start = 0
    for member in small + (up_bias,):
        cuts.append(sums[start : start + member.shape[0]])
        start += member.shape[0]
    return (
        block_out.reshape(inputs.shape),
        input_grad.reshape(inputs.shape),
        cuts[0],
        cuts[1],
        qkv_grads,
        cuts[2],
        out_grads,
        cuts[3],
        cuts[4],
        cuts[5],
        up_grad,
        cuts[7],
        down_grad,
        cuts[6],
    )


def solution(mesh):
    placed = (
        P(None, "dp", "ctx", None),
        P(None, "dp", None),
        P("dp"),
        P("dp"),
        P("ctx", "dp"),
        P("dp"),
        P("ctx", "dp"),
        P("dp"),
        P("dp"),
        P("dp"),
        P("ctx", "dp"),
        P("dp"),
        P("ctx", "dp"),
        P("dp"),
        P(None, "dp", "ctx", None),
    )
    return jax.shard_map(
        local,
        mesh=mesh,
        in_specs=placed,
        out_specs=(
            P(None, "dp", "ctx", None),
            P(None, "dp", "ctx", None),
            P("dp"),
            P("dp"),
            P("ctx", "dp"),
            P("dp"),
            P("ctx", "dp"),
            P("dp"),
            P("dp"),
            P("dp"),
            P("ctx", "dp"),
            P("dp"),
            P("ctx", "dp"),
            P("dp"),
        ),
        check_vma=False,
    )
```

time: 1390 us -> 961 us (0.69)
  starting transfers between devices: 423 us -> 41.7 us
  matrix products: 265 us -> 82.1 us
  waiting for transfers between devices: 377 us -> 522 us
  local copies, waits for them, and re-layouts: 129 us -> 173 us
  other arithmetic: 64.8 us -> 35.2 us
    ppermute x69 -> x2, starting transfers between devices: 422 us -> 5.44 us  [the longest x1 3.82 us: local(): down_piece = lax.ppermute(down_piece, ('dp', 'ctx'), route)]
    all_gather x6 -> x8, waiting for transfers between devices: 78.9 us -> 241 us  [the longest x1 65.9 us: local(): lax.all_gather(qkv[:, width:].reshape(micro, span, 2 * width), 'ctx', axi...]
    unnamed x19 -> x23, waiting for transfers between devices: 112 us -> 221 us
    reduce_scatter x3 -> x1, waiting for transfers between devices: 163 us -> 60.4 us  [local(): lax.psum_scatter(grad_kv, 'ctx', scatter_dimension=0)]
    reshape x6 -> x11, local copies, waits for them, and re-layouts: 4.68 us -> 96.1 us  [the longest x2 37.3 us: rows_first(): parts = per_head.reshape(micro, heads, devices, stream // devices, HEAD_DIM)]
    dot_general x12 -> x10, matrix products: 100 us -> 18.2 us  [outer_sum(): lax.dot_general(left, right, (((0,), (0,)), ((), ())), preferred_element_...]
    dot_general x180 -> x12, matrix products: 115 us -> 36.6 us  [the longest x7 28 us: dot32(): return jnp.dot(left, right, preferred_element_type=jnp.float32)]
    while x572 -> x0, local copies, waits for them, and re-layouts: 48 us -> none
  transfers between devices with their start and end apart: 83 -> 19, of which waited for: 30 -> 14; matrix products, arithmetic and copies ran while one was open for 22% -> 19% of each run, Pallas kernels for 0% -> 0%
where the time goes in v1:
time: 961 us; the launch traced here: 952 us
  waiting for transfers between devices  522 us (54%)
  local copies, waits for them, and re-layouts  173 us (18%)
  blocking collectives  83.3 us (9%)
  matrix products  82.1 us (9%)
  starting transfers between devices  41.7 us (4%)
  other arithmetic  35.2 us (4%)
  between operations  14.9 us (2%)
    unnamed x23, waiting for transfers between devices  221 us
    all_gather x1, waiting for transfers between devices, local(): lax.all_gather(qkv[:, width:].reshape(micro, span, 2 * width), 'ctx', axi...  65.9 us
    reduce_scatter x1, waiting for transfers between devices, local(): lax.psum_scatter(grad_kv, 'ctx', scatter_dimension=0)  60.4 us
    all_gather x1, waiting for transfers between devices, local(): lax.all_gather(lax.all_gather(w_qkv, 'ctx', axis=0, tiled=True), 'dp', ax...  53.3 us
    reshape x2, local copies, waits for them, and re-layouts, rows_first(): parts = per_head.reshape(micro, heads, devices, stream // devices, HEAD_DIM)  37.3 us
    all_to_all x1, starting transfers between devices, local(): lax.all_to_all(down_grad, 'dp', split_axis=1, concat_axis=0, tiled=True)  34.2 us
    all_gather x1, waiting for transfers between devices, local(): lax.all_gather(w_qkv, 'ctx', axis=0, tiled=True)  32.3 us
    dot_general x7, matrix products, dot32(): return jnp.dot(left, right, preferred_element_type=jnp.float32)  28 us
  transfers between devices with their start and end apart: 19, of which 14 were waited for; matrix products, arithmetic and copies ran while one was open for 19% of the time, Pallas kernels for 0%

profile of v1, /device:TPU:0, one launch (start us, length us, event | category | flops | bytes accessed | tf_op | source)
XLA Modules:
  0.0 951.8 jit_solution(14872864772454495306)
XLA Ops:
  8.0 32.3 %all-gather.15.cloned.1.call-done = bf16[1088,816]{1,0:T(8,128)(2,1)} async-done(((bf16[136,816]{1,0:T(8,128)(2,1)}), bf16[1088,816]{1,0:T(8,128)(2,1)}) %all-gather.15.cloned.1.call-update) | async-done | bytes 1775632 | tf_op jit(solution)/shard_map/all_gather | solution.py:123
  44.4 15.9 %all_gather.45 = bf16[1088,272]{1,0:T(8,128)(2,1)S(1)} all-gather(bf16[136,272]{1,0:T(8,128)(2,1)S(1)} %copy-done.25), channel_id=1, replica_groups=mesh['dp'=4,'ctx'=8] {'ctx'}, dimensions={0}, use_global_device_ids=true | all-gather | bytes 665856 | tf_op jit(solution)/shard_map/all_gather | solution.py:124
  71.3 53.3 %all-gather.27.cloned.1.call-done = bf16[4,1088,816]{1,2,0:T(8,128)(2,1)} async-done(((bf16[1,1088,816]{1,2,0:T(8,128)(2,1)}), bf16[4,1088,816]{1,2,0:T(8,128)(2,1)}) %all-gather.27.cloned.1.call-update) | async-done | bytes 7102480 | tf_op jit(solution)/shard_map/all_gather | solution.py:123
  144.4 21.5 %all-gather.29.cloned.1.call-done = bf16[4,1088,272]{1,2,0:T(8,128)(2,1)} async-done(((bf16[1,1088,272]{1,2,0:T(8,128)(2,1)}), bf16[4,1088,272]{1,2,0:T(8,128)(2,1)}) %all-gather.29.cloned.1.call-update) | async-done | bytes 2367504 | tf_op jit(solution)/shard_map/all_gather | solution.py:124
  169.6 65.9 %all-gather.17.cloned.1.call-done = bf16[8,3,64,2176]{3,2,1,0:T(8,128)(2,1)} async-done(((bf16[1,3,64,2176]{3,2,1,0:T(8,128)(2,1)}), bf16[8,3,64,2176]{3,2,1,0:T(8,128)(2,1)}) %all-gather.17.cloned.1.call-update) | async-done | bytes 6684688 | tf_op jit(solution)/shard_map/all_gather | solution.py:138
  235.4 20.3 %reshape.367 = bf16[8,3,64,34,64]{4,3,2,1,0:T(8,128)(2,1)} reshape(bf16[8,3,64,2176]{3,2,1,0:T(8,128)(2,1)} %all-gather.17.cloned.1.call-done) | data formatting | bytes 13369344 | tf_op jit(solution)/shard_map/reshape | solution.py:51
  255.7 20.6 %copy.132 = bf16[3,34,8,64,64]{3,2,4,1,0:T(8,128)(2,1)} copy(bf16[3,34,8,64,64]{4,1,3,0,2:T(8,128)(2,1)} %bitcast.161) | data formatting | bytes 13369344 | tf_op jit(solution)/shard_map/transpose | solution.py:52
  276.3 18.3 %reshape.368 = bf16[3,34,512,64]{2,3,1,0:T(8,128)(2,1)} reshape(bf16[3,34,8,64,64]{3,2,4,1,0:T(8,128)(2,1)} %copy.132) | data formatting | bytes 13369344 | tf_op jit(solution)/shard_map/reshape | solution.py:53
  321.6 16.2 %all_to_all.32 = bf16[4,136,272]{2,1,0:T(8,128)(2,1)S(1)} all-to-all(bf16[4,136,272]{2,1,0:T(8,128)(2,1)} %bitcast.184), channel_id=1, replica_groups=mesh['dp'=4,'ctx'=8] {'dp'}, dimensions={0} | all-to-all | bytes 591872 | tf_op jit(solution)/shard_map/all_to_all | solution.py:127
  345.7 13.5 %all-gather.19.cloned.1.call-done = bf16[768,1088]{1,0:T(8,128)(2,1)} async-done(((bf16[192,1088]{1,0:T(8,128)(2,1)}), bf16[768,1088]{1,0:T(8,128)(2,1)}) %all-gather.19.cloned.1.call-update) | async-done | bytes 1671184 | tf_op jit(solution)/shard_map/all_gather | solution.py:158
  365.6 27.3 %all-gather.23.cloned.1.call-done = bf16[1088,1088]{1,0:T(8,128)(2,1)} async-done(((bf16[136,1088]{1,0:T(8,128)(2,1)}), bf16[1088,1088]{1,0:T(8,128)(2,1)}) %all-gather.23.cloned.1.call-update) | async-done | bytes 2367504 | tf_op jit(solution)/shard_map/all_gather | solution.py:130
  399.4 27.0 %all-gather.25.cloned.1.call-done = bf16[768,1088]{1,0:T(8,128)(2,1)} async-done(((bf16[192,1088]{1,0:T(8,128)(2,1)}), bf16[768,1088]{1,0:T(8,128)(2,1)}) %all-gather.25.cloned.1.call-update) | async-done | bytes 1671184 | tf_op jit(solution)/shard_map/all_gather | solution.py:131
  445.0 45.4 %reduce-scatter.25.cloned.1.call-done = bf16[1,192,2176]{2,1,0:T(8,128)(2,1)} async-done(((bf16[4,192,2176]{2,1,0:T(8,128)(2,1)}), bf16[1,192,2176]{2,1,0:T(8,128)(2,1)}) %reduce-scatter.25.cloned.1.call-update) | async-done | bytes 835600
  514.7 17.3 %reshape.375 = bf16[3,34,8,64,64]{3,2,4,1,0:T(8,128)(2,1)} reshape(bf16[3,34,512,64]{2,3,1,0:T(8,128)(2,1)} %pad_maximum_fusion.1) | data formatting | bytes 13369344 | tf_op jit(solution)/shard_map/reshape | solution.py:58
  532.0 19.9 %copy.142 = bf16[3,34,8,64,64]{4,1,3,0,2:T(8,128)(2,1)} copy(bf16[3,34,8,64,64]{3,2,4,1,0:T(8,128)(2,1)} %reshape.375) | data formatting | bytes 13369344 | tf_op jit(solution)/shard_map/reshape | solution.py:58
  551.9 19.8 %reshape.376 = bf16[8,3,64,2176]{3,2,1,0:T(8,128)(2,1)} reshape(bf16[8,3,64,34,64]{4,3,2,1,0:T(8,128)(2,1)} %bitcast.162) | data formatting | bytes 13369344 | tf_op jit(solution)/shard_map/reshape | solution.py:60
  585.1 60.4 %reduce-scatter.23.cloned.1.call-done = bf16[1,3,64,2176]{3,2,1,0:T(8,128)(2,1)} async-done(((bf16[8,3,64,2176]{3,2,1,0:T(8,128)(2,1)}), bf16[1,3,64,2176]{3,2,1,0:T(8,128)(2,1)}) %reduce-scatter.23.cloned.1.call-update) | async-done | bytes 835600 | tf_op jit(solution)/shard_map/reduce_scatter | solution.py:205
  688.4 81.8 %reduce-scatter.27.cloned.1.call-done = bf16[1,1088,816]{1,2,0:T(8,128)(2,1)} async-done(((bf16[4,1088,816]{1,2,0:T(8,128)(2,1)}), bf16[1,1088,816]{1,2,0:T(8,128)(2,1)}) %reduce-scatter.27.cloned.1.call-update) | async-done | bytes 1775632
  774.2 37.0 %reduce-scatter.37.cloned.1.call-done = bf16[136,1088]{1,0:T(8,128)(2,1)} async-done(((bf16[1088,1088]{1,0:T(8,128)(2,1)}), bf16[136,1088]{1,0:T(8,128)(2,1)}) %reduce-scatter.37.cloned.1.call-update) | async-done | bytes 295952
  814.0 34.2 %all-to-all-start.1 = ((bf16[136,4,272]{2,0,1:T(8,128)(2,1)}), bf16[136,4,272]{2,0,1:T(8,128)(2,1)S(1)}, u32[]{:S(2)}, u32[]{:S(2)}) async-start(bf16[136,4,272]{2,0,1:T(8,128)(2,1)} %copy.145), calls=%async_computation.2 | async-start | bytes 835584 | tf_op jit(solution)/shard_map/all_to_all | solution.py:179
  848.9 12.5 %reduce-scatter.35.cloned.1.call-done = bf16[136,1088]{1,0:T(8,128)(2,1)} async-done(((bf16[1088,1088]{1,0:T(8,128)(2,1)}), bf16[136,1088]{1,0:T(8,128)(2,1)}) %reduce-scatter.35.cloned.1.call-update) | async-done | bytes 295952
  864.7 30.5 %reduce-scatter.33.cloned.1.call-done = bf16[1,136,272]{2,1,0:T(8,128)(2,1)} async-done(((bf16[8,136,272]{2,1,0:T(8,128)(2,1)}), bf16[1,136,272]{2,1,0:T(8,128)(2,1)}) %reduce-scatter.33.cloned.1.call-update) | async-done | bytes 74000
  897.7 16.9 %all-reduce.1 = f32[4,2176]{1,0:T(4,128)S(1)} all-reduce(f32[4,2176]{1,0:T(4,128)S(1)} %concatenate.45), channel_id=7, replica_groups=mesh['dp'=4,'ctx'=8] {'dp'}, use_global_device_ids=true, to_apply=%region_23.24.clone | all-reduce | flops 8704 | bytes 69632
  915.3 26.1 %psum.7 = f32[3264]{0:T(1024)S(1)} all-reduce(f32[3264]{0:T(1024)S(1)} %pad_maximum_fusion.8), channel_id=1, replica_groups=mesh['dp'=4,'ctx'=8] {'ctx'}, use_global_device_ids=true, to_apply=%region_25.26 | all-reduce | flops 3264 | bytes 26112 | tf_op jit(solution)/shard_map/psum | solution.py:234
  (249 shorter events, 203.0 us)
Async XLA Ops:
  7.2 37.2 %copy-start.25 = (bf16[136,272]{1,0:T(8,128)(2,1)S(1)}, bf16[136,272]{1,0:T(8,128)(2,1)}, u32[]{:S(2)}) copy-start(bf16[136,272]{1,0:T(8,128)(2,1)} %param.21) | copy-start | bytes 221956
  7.2 33.1 %all-gather.15.cloned.1.call-start = ((), (), s32[]{:S(2)}) async-start(), calls=%async_computation.10 | async-start | bytes 2193408 | tf_op jit(solution)/shard_map/all_gather | solution.py:123
  7.9 116.7 %all-gather.27.cloned.1.call-start = ((), (), s32[]{:S(2)}) async-start(), calls=%async_computation.17 | async-start | bytes 9400320 | tf_op jit(solution)/shard_map/all_gather | solution.py:123
  44.3 121.6 %all-gather.29.cloned.1.call-start = ((), (), s32[]{:S(2)}) async-start(), calls=%async_computation.18 | async-start | bytes 3133440 | tf_op jit(solution)/shard_map/all_gather | solution.py:124
  61.4 174.0 %all-gather.17.cloned.1.call-start = ((), (), s32[]{:S(2)}) async-start(), calls=%async_computation.11 | async-start | bytes 7520256 | tf_op jit(solution)/shard_map/all_gather | solution.py:138
  142.3 203.3 %all-gather.21.cloned.1.call-start = ((), (), s32[]{:S(2)}) async-start(), calls=%async_computation.13 | async-start | bytes 2820096 | tf_op jit(solution)/shard_map/all_gather | solution.py:126
  142.9 216.3 %all-gather.19.cloned.1.call-start = ((), (), s32[]{:S(2)}) async-start(), calls=%async_computation.12 | async-start | bytes 2211840 | tf_op jit(solution)/shard_map/all_gather | solution.py:158
  169.5 125.1 %copy-start.15 = (bf16[1,3,64,17,64]{4,3,2,1,0:T(8,128)(2,1)}, bf16[1,3,64,17,64]{4,3,2,1,0:T(8,128)(2,1)S(1)}, u32[]{:S(2)}) copy-start(bf16[1,3,64,17,64]{4,3,2,1,0:T(8,128)(2,1)S(1)} %reshape_reshape.12) | copy-start | bytes 1253380
  317.6 28.0 %copy-start.26 = (bf16[1088]{0:T(1024)(128)(2,1)S(1)}, bf16[1088]{0:T(1024)(128)(2,1)}, u32[]{:S(2)}) copy-start(bf16[1088]{0:T(1024)(128)(2,1)} %param.26) | copy-start | bytes 6532
  319.6 73.2 %all-gather.23.cloned.1.call-start = ((), (), s32[]{:S(2)}) async-start(), calls=%async_computation.14 | async-start | bytes 2820096 | tf_op jit(solution)/shard_map/all_gather | solution.py:130
  340.8 3.8 collective-permute-start
  344.6 81.7 %all-gather.25.cloned.1.call-start = ((), (), s32[]{:S(2)}) async-start(), calls=%async_computation.15 | async-start | bytes 2211840 | tf_op jit(solution)/shard_map/all_gather | solution.py:131
  345.4 145.0 %reduce-scatter.25.cloned.1.call-start = ((), (), s32[]{:S(2)}) async-start(), calls=%async_computation.19 | async-start | bytes 4177920
  444.6 200.8 %reduce-scatter.23.cloned.1.call-start = ((), (), s32[]{:S(2)}) async-start(), calls=%async_computation.16 | async-start | bytes 7520256 | tf_op jit(solution)/shard_map/reduce_scatter | solution.py:205
  571.8 114.3 %reduce-scatter.31.cloned.1.call-start = ((), (), s32[]{:S(2)}) async-start(), calls=%async_computation.22 | async-start | bytes 3133440
  582.9 187.3 %reduce-scatter.27.cloned.1.call-start = ((), (), s32[]{:S(2)}) async-start(), calls=%async_computation.20 | async-start | bytes 9400320
  661.5 149.7 %reduce-scatter.37.cloned.1.call-start = ((), (), s32[]{:S(2)}) async-start(), calls=%async_computation.25 | async-start | bytes 2820096
  668.8 192.7 %reduce-scatter.35.cloned.1.call-start = ((), (), s32[]{:S(2)}) async-start(), calls=%async_computation.24 | async-start | bytes 2820096
  674.8 220.4 %reduce-scatter.33.cloned.1.call-start = ((), (), s32[]{:S(2)}) async-start(), calls=%async_computation.23 | async-start | bytes 940032
  688.4 159.8 %copy-start.13 = (bf16[3,1,64,1088]{3,2,1,0:T(8,128)(2,1)S(1)}, bf16[3,1,64,1088]{3,2,1,0:T(8,128)(2,1)}, u32[]{:S(2)}) copy-start(bf16[3,1,64,1088]{3,2,1,0:T(8,128)(2,1)} %param.29) | copy-start | bytes 1253380
  688.4 255.0 %reduce-scatter.29.cloned.1.call-start = ((), (), s32[]{:S(2)}) async-start(), calls=%async_computation.21 | async-start | bytes 2193408
  774.2 74.2 %copy-start.36 = (u32[32]{0:T(128)S(1)}, u32[32]{0:T(128)}, u32[]{:S(2)}) copy-start(u32[32]{0:T(128)} %constant.51) | copy-start | bytes 388
  811.2 1.6 collective-permute-start.1
  814.0 49.2 %all-to-all-start.1 = ((bf16[136,4,272]{2,0,1:T(8,128)(2,1)}), bf16[136,4,272]{2,0,1:T(8,128)(2,1)S(1)}, u32[]{:S(2)}, u32[]{:S(2)}) async-start(bf16[136,4,272]{2,0,1:T(8,128)(2,1)} %copy.145), calls=%async_computation.2 | async-start | bytes 835584 | tf_op jit(solution)/shard_map/all_to_all | solution.py:179
  (36 other events, 257.2 us)
Sparse Core Ops, SparseCore 0:
  9.7 30.5 all-gather.14
  44.5 80.1 all-gather.26
  127.1 38.7 all-gather.28
  167.4 67.9 all-gather.16
  236.9 31.4 all-gather.20
  319.8 39.3 all-gather.18
  360.8 31.9 all-gather.22
  394.7 31.6 all-gather.24
  444.8 45.5 reduce-scatter.24
  571.9 73.5 reduce-scatter.22
  648.8 37.2 reduce-scatter.30
  688.9 81.2 reduce-scatter.26
  772.6 38.5 reduce-scatter.36
  813.4 47.9 reduce-scatter.34
  863.7 31.5 reduce-scatter.32
  897.4 36.8 reduce-scatter.28

commit v2 on v1

v2 whole, which is shorter than its diff:
```python
import jax
import jax.numpy as jnp
from jax import lax
from jax.experimental import pallas as pl
from jax.experimental.pallas import tpu as pltpu
from jax.sharding import PartitionSpec as P

HEADS = 17
HEAD_DIM = 64
PAIR = 2 * HEAD_DIM
PAIRS = (HEADS + 1) // 2


EPSILON = 1e-05
SCALE = 0.125
NEGATIVE = -1e30


def layer_norm(values, scale, shift):
    row_mean = jnp.mean(values, axis=-1, keepdims=True)
    centered = values - row_mean
    variance = jnp.mean(centered * centered, axis=-1, keepdims=True)
    inverse = lax.rsqrt(variance + EPSILON)
    normal = centered * inverse
    return (normal * scale + shift, normal, inverse)


def norm_back(grad_normed, normal, inverse, scale):
    scaled = grad_normed * scale
    return inverse * (
        scaled
        - jnp.mean(scaled, axis=-1, keepdims=True)
        - normal * jnp.mean(scaled * normal, axis=-1, keepdims=True)
    )


def outer_sum(left, right):
    return lax.dot_general(
        left, right, (((0,), (0,)), ((), ())), preferred_element_type=jnp.float32
    )


def back_dot(gradient, weight):
    return lax.dot_general(
        gradient, weight, (((1,), (1,)), ((), ())), preferred_element_type=jnp.float32
    )


def head_part(block, half):
    lane = lax.broadcasted_iota(jnp.int32, block.shape, 1)
    return jnp.where(lane // HEAD_DIM == half, block.astype(jnp.float32), 0.0).astype(block.dtype)


def joined(first, second):
    lane = lax.broadcasted_iota(jnp.int32, first.shape, 1)
    return jnp.where(lane < HEAD_DIM, first, second)


def attend_kernel(first_ref, last_ref, q_ref, kv_ref, out_ref, weights_ref):
    stream = weights_ref.shape[3]
    keys = kv_ref[:, 0, 0].reshape(stream, PAIR)
    values = kv_ref[:, 0, 1].reshape(stream, PAIR)
    key_pos = lax.broadcasted_iota(jnp.int32, (q_ref.shape[1], stream), 1)
    visible = (key_pos >= first_ref[0]) & (key_pos <= last_ref[0])
    attended = []
    for half in range(2):
        scores = back_dot(head_part(q_ref[0], half), keys) * SCALE
        scores = jnp.where(visible, scores, NEGATIVE)
        weights = jnp.exp(scores - jnp.max(scores, axis=1, keepdims=True))
        weights = weights / jnp.sum(weights, axis=1, keepdims=True)
        weights = weights.astype(jnp.bfloat16)
        weights_ref[0, half] = weights
        attended.append(dot32(weights, values))
    out_ref[0] = joined(*attended).astype(jnp.bfloat16)


def attend_back_kernel(q_ref, kv_ref, grad_ref, weights_ref, grad_q_ref, grad_kv_ref):
    stream = weights_ref.shape[3]
    keys = kv_ref[:, 0, 0].reshape(stream, PAIR)
    values = kv_ref[:, 0, 1].reshape(stream, PAIR)
    grad_q = []
    grad_k = jnp.zeros((stream, PAIR), jnp.float32)
    grad_v = jnp.zeros((stream, PAIR), jnp.float32)
    for half in range(2):
        weights = weights_ref[0, half]
        weights32 = weights.astype(jnp.float32)
        grad = head_part(grad_ref[0], half)
        grad_weights = back_dot(grad, values)
        row_dot = jnp.sum(weights32 * grad_weights, axis=1, keepdims=True)
        grad_scores = (weights32 * (grad_weights - row_dot)).astype(jnp.bfloat16)
        grad_q.append(dot32(grad_scores, keys))
        grad_k = grad_k + outer_sum(grad_scores, head_part(q_ref[0], half))
        grad_v = grad_v + outer_sum(weights, grad)
    grad_q_ref[0] = (joined(*grad_q) * SCALE).astype(jnp.bfloat16)
    block = grad_kv_ref.shape
    grad_kv_ref[:, 0, 0] = (grad_k * SCALE).astype(jnp.bfloat16).reshape(block[0], block[3], PAIR)
    grad_kv_ref[:, 0, 1] = grad_v.astype(jnp.bfloat16).reshape(block[0], block[3], PAIR)


def attention_specs(span, ctx_size):
    row = pl.BlockSpec((1, span, PAIR), lambda m, p: (m, 0, p))
    kv = pl.BlockSpec((ctx_size, 1, 2, span, PAIR), lambda m, p: (0, m, 0, 0, p))
    weights = pl.BlockSpec((1, 2, span, ctx_size * span), lambda m, p: (m, p, 0, 0))
    limit = pl.BlockSpec((1, span, 1), lambda m, p: (m, 0, 0))
    return row, kv, weights, limit


def attend(first, last, queries, kv_all):
    ctx_size, micro, _, span, padded = kv_all.shape
    row, kv, weights, limit = attention_specs(span, ctx_size)
    return pl.pallas_call(
        attend_kernel,
        grid=(micro, PAIRS),
        in_specs=[limit, limit, row, kv],
        out_specs=[row, weights],
        out_shape=[
            jax.ShapeDtypeStruct((micro, span, padded), jnp.bfloat16),
            jax.ShapeDtypeStruct((micro, 2 * PAIRS, span, ctx_size * span), jnp.bfloat16),
        ],
        compiler_params=pltpu.CompilerParams(vmem_limit_bytes=24 * 2**20),
    )(first, last, queries, kv_all)


def attend_back(queries, kv_all, grad, weights_all):
    ctx_size, micro, _, span, padded = kv_all.shape
    row, kv, weights, _ = attention_specs(span, ctx_size)
    return pl.pallas_call(
        attend_back_kernel,
        grid=(micro, PAIRS),
        in_specs=[row, kv, row, weights],
        out_specs=[row, kv],
        out_shape=[
            jax.ShapeDtypeStruct((micro, span, padded), jnp.bfloat16),
            jax.ShapeDtypeStruct(kv_all.shape, jnp.bfloat16),
        ],
        compiler_params=pltpu.CompilerParams(vmem_limit_bytes=24 * 2**20),
    )(queries, kv_all, grad, weights_all)


def padded_heads(rows, micro):
    rows = jnp.pad(rows, ((0, 0), (0, PAIRS * PAIR - rows.shape[1])))
    return rows.reshape(micro, -1, PAIRS * PAIR)


def plain_heads(rows, width):
    return rows.reshape(-1, rows.shape[-1])[:, :width]


def shared(block):
    count = lax.axis_size("dp")
    return [block] + [
        lax.ppermute(block, "dp", [(s, (s + k) % count) for s in range(count)])
        for k in range(1, count)
    ]


def returned(blocks):
    count = lax.axis_size("dp")
    total = blocks[0].astype(jnp.float32)
    for k in range(1, count):
        route = [(s, (s - k) % count) for s in range(count)]
        total = total + lax.ppermute(blocks[k], "dp", route).astype(jnp.float32)
    return total


def swapped(blocks, start, step):
    stacked = jnp.stack(blocks)
    count = len(blocks)
    return [
        lax.dynamic_index_in_dim(stacked, (start + step * j) % count, 0, keepdims=False)
        for j in range(count)
    ]


def dot32(left, right):
    return jnp.dot(left, right, preferred_element_type=jnp.float32)


def piece_route(k, dp_size, ctx_size):
    return [
        (d * ctx_size + r, r * dp_size + (d + k) % dp_size)
        for d in range(dp_size)
        for r in range(ctx_size)
    ]


def local(
    inputs,
    lengths,
    ln1_scale,
    ln1_bias,
    w_qkv,
    qv_bias,
    w_out,
    out_bias,
    ln2_scale,
    ln2_bias,
    w_up,
    up_bias,
    w_down,
    down_bias,
    out_grad,
):
    ctx_index = lax.axis_index("ctx")
    ctx_size = lax.axis_size("ctx")
    dp_index = lax.axis_index("dp")
    dp_size = lax.axis_size("dp")
    piece_index = (dp_index * ctx_size + ctx_index) % dp_size
    micro, _, span, width = inputs.shape
    rows = micro * span
    qkv_part = w_qkv.shape[1]
    out_part = w_out.shape[1]
    bf16 = jnp.bfloat16
    f32 = jnp.float32

    tokens32 = inputs.reshape(rows, width).astype(f32)
    grad_out = out_grad.reshape(rows, width)
    grad32 = grad_out.astype(f32)

    small = (ln1_scale, ln1_bias, qv_bias, out_bias, ln2_scale, ln2_bias, down_bias)
    small_all = lax.all_gather(jnp.concatenate(small), "dp", axis=0)
    vectors = []
    start = 0
    for member in small:
        size = member.shape[0]
        vectors.append(small_all[:, start : start + size].reshape(-1).astype(f32))
        start += size
    ln1_scale, ln1_bias, qv_bias, out_bias, ln2_scale, ln2_bias, down_bias = vectors
    qkv_near = shared(lax.all_gather(w_qkv, "ctx", axis=0, tiled=True))
    out_near = shared(lax.all_gather(w_out, "ctx", axis=0, tiled=True))
    grad_all = jnp.concatenate(shared(grad_out), axis=0)
    up_here = lax.all_gather(w_up, "ctx", axis=0, tiled=True)
    down_rows = w_down.reshape(dp_size, -1, out_part)
    down_piece = [
        lax.ppermute(
            lax.dynamic_index_in_dim(down_rows, (dp_index + k) % dp_size, 0, keepdims=False),
            ("dp", "ctx"),
            piece_route(k, dp_size, ctx_size),
        )
        for k in range(dp_size)
    ]
    down_piece = jnp.concatenate(swapped(down_piece, piece_index, -1), axis=1)
    down_here = lax.all_gather(down_piece, "ctx", axis=0, tiled=True)

    normed1, normal1, inverse1 = layer_norm(tokens32, ln1_scale, ln1_bias)
    normed1 = normed1.astype(bf16)
    qkv_bias = jnp.concatenate([qv_bias[:width], jnp.zeros((width,), f32), qv_bias[width:]])
    qkv = swapped([dot32(normed1, piece) for piece in qkv_near], dp_index, -1)
    qkv = jnp.concatenate(qkv, axis=1)
    qkv = (qkv + qkv_bias).astype(bf16)
    queries = padded_heads(qkv[:, :width], micro)
    keys = padded_heads(qkv[:, width : 2 * width], micro)
    values = padded_heads(qkv[:, 2 * width :], micro)
    kv_all = lax.all_gather(jnp.stack([keys, values], axis=1), "ctx", axis=0)
    seq_ends = jnp.cumsum(lengths[:, 0], axis=1)
    last = ctx_index * span + jnp.arange(span, dtype=jnp.int32)
    last = jnp.broadcast_to(last[None, :, None], (micro, span, 1))
    ends = seq_ends[:, None, :]
    first = jnp.max(jnp.where(ends <= last, ends, 0), axis=2, keepdims=True).astype(jnp.int32)
    attended, weights = attend(first, last, queries, kv_all)
    attended = plain_heads(attended, width)
    branch = swapped([dot32(attended, piece) for piece in out_near], dp_index, -1)
    residual = tokens32 + jnp.concatenate(branch, axis=1) + out_bias
    normed2, normal2, inverse2 = layer_norm(residual, ln2_scale, ln2_bias)
    normed2_all = jnp.concatenate(shared(normed2.astype(bf16)), axis=0)

    gelu_input = dot32(normed2_all, up_here) + up_bias.astype(f32)
    hidden, gelu_pull = jax.vjp(jax.nn.gelu, gelu_input)
    hidden = hidden.astype(bf16)
    grad_upper = gelu_pull(back_dot(grad_all, down_here))[0].astype(bf16)
    both = jnp.concatenate(
        [dot32(hidden, down_here).astype(bf16), back_dot(grad_upper, up_here).astype(bf16)], axis=1
    )
    both = returned([both[k * rows : (k + 1) * rows] for k in range(dp_size)])
    block_out = (residual + both[:, :width] + down_bias).astype(bf16)
    grad_normed2 = both[:, width:]
    up_grad = lax.psum_scatter(
        outer_sum(normed2_all, grad_upper).astype(bf16).reshape(ctx_size, -1, up_here.shape[1]),
        "ctx",
        scatter_dimension=0,
    ).astype(f32)
    down_grad = lax.psum_scatter(
        outer_sum(hidden, grad_all).astype(bf16).reshape(ctx_size, -1, width),
        "ctx",
        scatter_dimension=0,
    )
    down_cols = [down_grad[:, j * out_part : (j + 1) * out_part] for j in range(dp_size)]
    down_cols = swapped(down_cols, piece_index, -1)
    down_grad = [
        lax.ppermute(
            down_cols[k], ("dp", "ctx"), [(b, a) for a, b in piece_route(k, dp_size, ctx_size)]
        )
        for k in range(dp_size)
    ]
    down_grad = jnp.concatenate(swapped(down_grad, -dp_index, 1), axis=0).astype(f32)

    grad_residual = grad32 + norm_back(grad_normed2, normal2, inverse2, ln2_scale)
    grad_branch = grad_residual.astype(bf16)
    branch_parts = [
        grad_branch[:, j * out_part : (j + 1) * out_part] for j in range(dp_size)
    ]
    branch_parts = swapped(branch_parts, dp_index, -1)
    grad_attended = back_dot(branch_parts[0], out_near[0])
    for k in range(1, dp_size):
        grad_attended = grad_attended + back_dot(branch_parts[k], out_near[k])
    grad_attended = padded_heads(grad_attended.astype(bf16), micro)
    out_grads = returned([outer_sum(attended, part).astype(bf16) for part in branch_parts])
    out_grads = out_grads.astype(bf16)
    out_grads = out_grads.reshape(ctx_size, -1, out_part)
    out_grads = lax.psum_scatter(out_grads, "ctx", scatter_dimension=0).astype(f32)
    grad_queries, grad_kv = attend_back(queries, kv_all, grad_attended, weights)
    grad_kv = lax.psum_scatter(grad_kv, "ctx", scatter_dimension=0)
    grad_qkv = jnp.concatenate(
        [
            plain_heads(grad_queries, width),
            plain_heads(grad_kv[:, 0], width),
            plain_heads(grad_kv[:, 1], width),
        ],
        axis=1,
    )
    pieces = [grad_qkv[:, j * qkv_part : (j + 1) * qkv_part] for j in range(dp_size)]
    pieces = swapped(pieces, dp_index, -1)
    qkv_grads = returned([outer_sum(normed1, piece).astype(bf16) for piece in pieces])
    grad_normed1 = back_dot(pieces[0], qkv_near[0])
    for j in range(1, dp_size):
        grad_normed1 = grad_normed1 + back_dot(pieces[j], qkv_near[j])
    input_grad = (grad_residual + norm_back(grad_normed1, normal1, inverse1, ln1_scale)).astype(
        bf16
    )

    qkv_sums = jnp.sum(grad_qkv.astype(f32), axis=0)
    sums = (
        jnp.sum(grad_normed1 * normal1, axis=0),
        jnp.sum(grad_normed1, axis=0),
        jnp.concatenate([qkv_sums[:width], qkv_sums[2 * width :]]),
        jnp.sum(grad_branch.astype(f32), axis=0),
        jnp.sum(grad_normed2 * normal2, axis=0),
        jnp.sum(grad_normed2, axis=0),
        jnp.sum(grad32, axis=0),
    )
    sums = jnp.concatenate([member.reshape(dp_size, -1) for member in sums], axis=1)
    sums = returned(swapped([sums[j] for j in range(dp_size)], dp_index, -1))
    up_sums = jnp.sum(grad_upper.astype(f32), axis=0)
    sums = jnp.concatenate([sums, up_sums]).reshape(-1, qkv_part)
    sums = jnp.pad(sums, ((0, 8 - sums.shape[0]), (0, 0)))
    sums = jnp.broadcast_to(sums[None], (ctx_size,) + sums.shape)
    qkv_rows = width // ctx_size
    qkv_grads = jnp.concatenate([qkv_grads.reshape(ctx_size, qkv_rows, qkv_part), sums], axis=1)
    qkv_grads = lax.psum_scatter(qkv_grads.astype(bf16), "ctx", scatter_dimension=0).astype(f32)
    sums = qkv_grads[qkv_rows:].reshape(-1)
    qkv_grads = qkv_grads[:qkv_rows]
    cuts = []
    start = 0
    for member in small + (up_bias,):
        cuts.append(sums[start : start + member.shape[0]])
        start += member.shape[0]
    return (
        block_out.reshape(inputs.shape),
        input_grad.reshape(inputs.shape),
        cuts[0],
        cuts[1],
        qkv_grads,
        cuts[2],
        out_grads,
        cuts[3],
        cuts[4],
        cuts[5],
        up_grad,
        cuts[7],
        down_grad,
        cuts[6],
    )


def solution(mesh):
    placed = (
        P(None, "dp", "ctx", None),
        P(None, "dp", None),
        P("dp"),
        P("dp"),
        P("ctx", "dp"),
        P("dp"),
        P("ctx", "dp"),
        P("dp"),
        P("dp"),
        P("dp"),
        P("ctx", "dp"),
        P("dp"),
        P("ctx", "dp"),
        P("dp"),
        P(None, "dp", "ctx", None),
    )
    return jax.shard_map(
        local,
        mesh=mesh,
        in_specs=placed,
        out_specs=(
            P(None, "dp", "ctx", None),
            P(None, "dp", "ctx", None),
            P("dp"),
            P("dp"),
            P("ctx", "dp"),
            P("dp"),
            P("ctx", "dp"),
            P("dp"),
            P("dp"),
            P("dp"),
            P("ctx", "dp"),
            P("dp"),
            P("ctx", "dp"),
            P("dp"),
        ),
        check_vma=False,
    )
```

time: 961 us -> 653 us (0.68)
  waiting for transfers between devices: 522 us -> 328 us
  local copies, waits for them, and re-layouts: 173 us -> 53.4 us
  Pallas kernels: 0 us -> 48.8 us
  blocking collectives: 83.3 us -> 44.6 us
  starting transfers between devices: 41.7 us -> 56.6 us
  matrix products: 82.1 us -> 69.1 us
    ppermute x2 -> x32, waiting for transfers between devices: 0.01 us -> 247 us  [the longest x12 121 us: returned(): total = total + lax.ppermute(blocks[k], 'dp', route).astype(jnp.float32)]
    unnamed x23 -> x12, waiting for transfers between devices: 221 us -> 1.52 us
    all_gather x6 -> x2, waiting for transfers between devices: 214 us -> 36.7 us  [the longest x1 20.2 us: local(): kv_all = lax.all_gather(jnp.stack([keys, values], axis=1), 'ctx', axis=0)]
    reshape x5 -> x2, local copies, waits for them, and re-layouts: 95.7 us -> 0.18 us  [the longest x1 0.09 us: local(): sums = jnp.concatenate([sums, up_sums]).reshape(-1, qkv_part)]
    ppermute x2 -> x32, starting transfers between devices: 5.44 us -> 56 us  [the longest x12 19.4 us: shared(): lax.ppermute(block, 'dp', [(s, (s + k) % count) for s in range(count)])]
    pallas_call x0 -> x2, Pallas kernels: none -> 48.8 us  [the longest x1 25.3 us: attend_back(): pl.pallas_call(attend_back_kernel, grid=(micro, PAIRS), in_specs=[row, kv...]
    all_to_all x1 -> x0, starting transfers between devices: 34.2 us -> none  [local(): lax.all_to_all(down_grad, 'dp', split_axis=1, concat_axis=0, tiled=True)]
    all_gather x1, waiting for transfers between devices: 27.3 us -> 0.01 us  [local(): down_here = lax.all_gather(down_piece, 'ctx', axis=0, tiled=True)]
  transfers between devices with their start and end apart: 19 -> 41, of which waited for: 14 -> 21; matrix products, arithmetic and copies ran while one was open for 19% -> 16% of each run, Pallas kernels for 0% -> 4%
where the time goes in v2:
time: 653 us; the launch traced here: 643 us
  waiting for transfers between devices  328 us (50%)
  matrix products  69.1 us (11%)
  starting transfers between devices  56.6 us (9%)
  local copies, waits for them, and re-layouts  53.4 us (8%)
  Pallas kernels  48.8 us (7%)
  blocking collectives  44.6 us (7%)
  other arithmetic  26.6 us (4%)
  between operations  15.5 us (2%)
    ppermute x12, waiting for transfers between devices, returned(): total = total + lax.ppermute(blocks[k], 'dp', route).astype(jnp.float32)  121 us
    ppermute x12, waiting for transfers between devices, shared(): lax.ppermute(block, 'dp', [(s, (s + k) % count) for s in range(count)])  97.6 us
    all_gather x1, blocking collectives, local(): out_near = shared(lax.all_gather(w_out, 'ctx', axis=0, tiled=True))  35 us
    reduce_scatter x1, waiting for transfers between devices, local(): grad_kv = lax.psum_scatter(grad_kv, 'ctx', scatter_dimension=0)  29.4 us
    pallas_call x1, Pallas kernels, attend_back(): pl.pallas_call(attend_back_kernel, grid=(micro, PAIRS), in_specs=[row, kv...  25.3 us
    dot_general x10, matrix products, outer_sum(): lax.dot_general(left, right, (((0,), (0,)), ((), ())), preferred_element_...  25 us
    pallas_call x1, Pallas kernels, attend(): pl.pallas_call(attend_kernel, grid=(micro, PAIRS), in_specs=[limit, limit...  23.6 us
    ppermute x4, waiting for transfers between devices, local(): lax.ppermute(down_cols[k], ('dp', 'ctx'), [(b, a) for a, b in piece_route...  23.6 us
  transfers between devices with their start and end apart: 41, of which 21 were waited for; matrix products, arithmetic and copies ran while one was open for 16% of the time, Pallas kernels for 4%

profile of v2, /device:TPU:0, one launch (start us, length us, event | category | flops | bytes accessed | tf_op | source)
XLA Modules:
  0.0 643.0 jit_solution(6998514014833474363)
XLA Ops:
  12.9 9.6 %all-gather.2 = bf16[4,1,2176]{2,1,0:T(2,128)(2,1)S(1)} all-gather(bf16[1,1,2176]{2,1,0:T(2,128)(2,1)S(1)} %reshape.426), channel_id=2, replica_groups=mesh['dp'=4,'ctx'=8] {'dp'}, dimensions={0}, use_global_device_ids=true | all-gather | bytes 21760 | tf_op jit(solution)/shard_map/all_gather | solution.py:221
  23.8 16.5 %all-gather.8.cloned.1.call-done = bf16[1088,816]{1,0:T(8,128)(2,1)} async-done(((bf16[136,816]{1,0:T(8,128)(2,1)}), bf16[1088,816]{1,0:T(8,128)(2,1)}) %all-gather.8.cloned.1.call-update) | async-done | bytes 1775632 | tf_op jit(solution)/shard_map/all_gather | solution.py:229
  51.8 36.6 %collective-permute-done.2 = bf16[1088,816]{0,1:T(8,128)(2,1)} collective-permute-done((bf16[1088,816]{0,1:T(8,128)(2,1)}, bf16[1088,816]{0,1:T(8,128)(2,1)}, u32[]{:S(2)}, u32[]{:S(2)}) %collective-permute-start.2) | collective-permute-done | bytes 1775648 | tf_op jit(solution)/shard_map/ppermute | solution.py:152
  90.7 39.4 %collective-permute-done.1 = bf16[1088,816]{0,1:T(8,128)(2,1)} collective-permute-done((bf16[1088,816]{0,1:T(8,128)(2,1)}, bf16[1088,816]{0,1:T(8,128)(2,1)}, u32[]{:S(2)}, u32[]{:S(2)}) %collective-permute-start.1) | collective-permute-done | bytes 1775648 | tf_op jit(solution)/shard_map/ppermute | solution.py:152
  159.0 35.0 %all_gather.29 = bf16[1088,272]{1,0:T(8,128)(2,1)S(1)} all-gather(bf16[136,272]{1,0:T(8,128)(2,1)S(1)} %copy-done.22), channel_id=1, replica_groups=mesh['dp'=4,'ctx'=8] {'ctx'}, dimensions={0}, use_global_device_ids=true | all-gather | bytes 665856 | tf_op jit(solution)/shard_map/all_gather | solution.py:230
  195.1 5.5 collective-permute-start.4
  204.3 20.2 %all-gather.14.cloned.1.call-done = bf16[24,2,64,1152]{3,2,1,0:T(8,128)(2,1)} async-done(((bf16[3,2,64,1152]{3,2,1,0:T(8,128)(2,1)}), bf16[24,2,64,1152]{3,2,1,0:T(8,128)(2,1)}) %all-gather.14.cloned.1.call-update) | async-done | bytes 7077904 | tf_op jit(solution)/shard_map/all_gather | solution.py:254
  227.6 23.6 %shard_map.254 = (bf16[3,64,1152]{2,1,0:T(8,128)(2,1)S(1)}, bf16[3,18,64,512]{3,2,1,0:T(8,128)(2,1)S(1)}) custom-call(s32[3,64,1]{2,1,0:T(8,128)S(1)} %copy.197.first_ref, s32[3,64,1]{2,1,0:T(8,128)S(1)} %broadcast_in_dim.20.last_ref, bf16[3,64,1152]{2,1,0:T(8,128)(2,1)S(1)} %bitcast.256, bf16[8,3,2,64,1152]{4,3,2,1,0:T(8,128)(2,1)S(1)} %bitcast.244), custom_call_target="tpu_custom_call" | custom-call | tf_op jit(solution)/shard_map/pallas_call | solution.py:111
  272.6 7.4 %collective-permute-done.8 = bf16[192,1088]{1,0:T(8,128)(2,1)} collective-permute-done((bf16[192,1088]{1,0:T(8,128)(2,1)}, bf16[192,1088]{1,0:T(8,128)(2,1)}, u32[]{:S(2)}, u32[]{:S(2)}) %collective-permute-start.8) | collective-permute-done | bytes 417824 | tf_op jit(solution)/shard_map/ppermute | solution.py:152
  282.5 7.9 %collective-permute-done.7 = bf16[192,1088]{1,0:T(8,128)(2,1)} collective-permute-done((bf16[192,1088]{1,0:T(8,128)(2,1)}, bf16[192,1088]{1,0:T(8,128)(2,1)}, u32[]{:S(2)}, u32[]{:S(2)}) %collective-permute-start.7) | collective-permute-done | bytes 417824 | tf_op jit(solution)/shard_map/ppermute | solution.py:152
  290.6 6.4 convolution_add_fusion
  297.0 5.6 convolution_convert_fusion.7
  322.5 18.2 %collective-permute-done.16 = bf16[192,2176]{1,0:T(8,128)(2,1)} collective-permute-done((bf16[192,2176]{1,0:T(8,128)(2,1)}, bf16[192,2176]{1,0:T(8,128)(2,1)}, u32[]{:S(2)}, u32[]{:S(2)}) %collective-permute-start.16) | collective-permute-done | bytes 835616 | tf_op jit(solution)/shard_map/ppermute | solution.py:162
  340.7 16.4 %collective-permute-done.18 = bf16[192,2176]{1,0:T(8,128)(2,1)} collective-permute-done((bf16[192,2176]{1,0:T(8,128)(2,1)}, bf16[192,2176]{1,0:T(8,128)(2,1)}, u32[]{:S(2)}, u32[]{:S(2)}) %collective-permute-start.18) | collective-permute-done | bytes 835616 | tf_op jit(solution)/shard_map/ppermute | solution.py:162
  368.2 25.3 %shard_map.255 = (bf16[3,64,1152]{2,1,0:T(8,128)(2,1)S(1)}, bf16[8,3,2,64,1152]{4,3,2,1,0:T(8,128)(2,1)S(1)}) custom-call(bf16[3,64,1152]{2,1,0:T(8,128)(2,1)S(1)} %bitcast.257, bf16[8,3,2,64,1152]{4,3,2,1,0:T(8,128)(2,1)S(1)} %bitcast.247, bf16[3,64,1152]{2,1,0:T(8,128)(2,1)S(1)} %bitcast.261, bf16[3,18,64,512]{3,2,1,0:T(8,128)(2,1)S(1)} %copy-done.3), custom_call_target="tpu_custom_call" | custom-call | tf_op jit(solution)/shard_map/pallas_call | solution.py:127
  401.1 14.5 %collective-permute-done.27 = bf16[1088,272]{0,1:T(8,128)(2,1)S(1)} collective-permute-done((bf16[1088,272]{0,1:T(8,128)(2,1)S(1)}, bf16[1088,272]{0,1:T(8,128)(2,1)S(1)}, u32[]{:S(2)}, u32[]{:S(2)}) %collective-permute-start.27) | collective-permute-done | bytes 591904 | tf_op jit(solution)/shard_map/ppermute | solution.py:162
  415.6 10.6 %collective-permute-done.26 = bf16[1088,272]{0,1:T(8,128)(2,1)S(1)} collective-permute-done((bf16[1088,272]{0,1:T(8,128)(2,1)S(1)}, bf16[1088,272]{0,1:T(8,128)(2,1)S(1)}, u32[]{:S(2)}, u32[]{:S(2)}) %collective-permute-start.26) | collective-permute-done | bytes 591904 | tf_op jit(solution)/shard_map/ppermute | solution.py:162
  428.1 6.8 %convolution_convert_fusion = bf16[1088,1088]{1,0:T(8,128)(2,1)} fusion(bf16[192,1088]{1,0:T(8,128)(2,1)} %collective-permute-done.15, bf16[192,1088]{1,0:T(8,128)(2,1)} %collective-permute-done.14, bf16[192,1088]{1,0:T(8,128)(2,1)} %collective-permute-done.13, bf16[192,1088]{1,0:T(8,128)(2,1)S(1)} %bitcast.289, f32[768,1088]{0,1:T(8,128)} %convolution_add_fusion), kind=kOutput, calls=%fused_computation | convolution fusion | flops 1833619456 | bytes 7380992 | tf_op jit(solution)/shard_map/dot_general | solution.py:38
  436.3 5.3 convolution_convert_fusion.1
  442.3 29.4 %reduce-scatter.12.cloned.1.call-done = bf16[1,3,2,64,1152]{4,3,2,1,0:T(8,128)(2,1)} async-done(((bf16[8,3,2,64,1152]{4,3,2,1,0:T(8,128)(2,1)}), bf16[1,3,2,64,1152]{4,3,2,1,0:T(8,128)(2,1)}) %reduce-scatter.12.cloned.1.call-update) | async-done | bytes 884752 | tf_op jit(solution)/shard_map/reduce_scatter | solution.py:312
  502.3 55.5 %collective-permute-done.22 = f32[2176]{0:T(1024)S(1)} collective-permute-done((f32[2176]{0:T(1024)S(1)}, f32[2176]{0:T(1024)S(1)}, u32[]{:S(2)}, u32[]{:S(2)}) %collective-permute-start.22) | collective-permute-done | bytes 8736 | tf_op jit(solution)/shard_map/ppermute | solution.py:162
  577.8 6.7 %collective-permute-start.31 = (bf16[136,272]{1,0:T(8,128)(2,1)S(1)}, bf16[136,272]{1,0:T(8,128)(2,1)S(1)}, u32[]{:S(2)}, u32[]{:S(2)}) collective-permute-start(bf16[136,272]{1,0:T(8,128)(2,1)S(1)} %get-tuple-element.170), channel_id=1, source_target_pairs={{3,0},{7,1},{11,2},{15,3},{19,4},{23,5},{27,6},{31,7},{0,8},{4,9},... | collective-permute-start | bytes 221960 | tf_op jit(solution)/shard_map/ppermute | solution.py:290
  591.4 19.7 %collective-permute-done.31 = bf16[136,272]{1,0:T(8,128)(2,1)S(1)} collective-permute-done((bf16[136,272]{1,0:T(8,128)(2,1)S(1)}, bf16[136,272]{1,0:T(8,128)(2,1)S(1)}, u32[]{:S(2)}, u32[]{:S(2)}) %collective-permute-start.31) | collective-permute-done | bytes 74016 | tf_op jit(solution)/shard_map/ppermute | solution.py:290
  617.8 13.6 %reduce-scatter.14.cloned.1.call-done = bf16[1,144,816]{2,1,0:T(8,128)(2,1)} async-done(((bf16[8,144,816]{2,1,0:T(8,128)(2,1)}), bf16[1,144,816]{2,1,0:T(8,128)(2,1)}) %reduce-scatter.14.cloned.1.call-update) | async-done | bytes 235024 | tf_op jit(solution)/shard_map/reduce_scatter | solution.py:349
  (304 shorter events, 191.8 us)
Async XLA Ops:
  7.2 33.1 %all-gather.8.cloned.1.call-start = ((), (), s32[]{:S(2)}) async-start(), calls=%async_computation.5 | async-start | bytes 2193408 | tf_op jit(solution)/shard_map/all_gather | solution.py:229
  7.9 216.6 %all-gather.14.cloned.1.call-start = ((), (), s32[]{:S(2)}) async-start(), calls=%async_computation.10 | async-start | bytes 7962624 | tf_op jit(solution)/shard_map/all_gather | solution.py:254
  44.2 44.1 %collective-permute-start.2 = (bf16[1088,816]{0,1:T(8,128)(2,1)}, bf16[1088,816]{0,1:T(8,128)(2,1)}, u32[]{:S(2)}, u32[]{:S(2)}) collective-permute-start(bf16[1088,816]{0,1:T(8,128)(2,1)} %copy.194), channel_id=1, source_target_pairs={{0,24},{8,0},{16,8},{24,16},{1,25},{9,1},{17,9},{25,17},{2,26},{10... | collective-permute-start | bytes 5326856 | tf_op jit(solution)/shard_map/ppermute | solution.py:152
  46.6 83.4 %collective-permute-start.1 = (bf16[1088,816]{0,1:T(8,128)(2,1)}, bf16[1088,816]{0,1:T(8,128)(2,1)}, u32[]{:S(2)}, u32[]{:S(2)}) collective-permute-start(bf16[1088,816]{0,1:T(8,128)(2,1)} %copy.194), channel_id=1, source_target_pairs={{0,16},{8,24},{16,0},{24,8},{1,17},{9,25},{17,1},{25,9},{2,18},{10... | collective-permute-start | bytes 5326856 | tf_op jit(solution)/shard_map/ppermute | solution.py:152
  47.4 84.9 %collective-permute-start = (bf16[1088,816]{0,1:T(8,128)(2,1)}, bf16[1088,816]{0,1:T(8,128)(2,1)}, u32[]{:S(2)}, u32[]{:S(2)}) collective-permute-start(bf16[1088,816]{0,1:T(8,128)(2,1)} %copy.194), channel_id=1, source_target_pairs={{0,8},{8,16},{16,24},{24,0},{1,9},{9,17},{17,25},{25,1},{2,10},{10... | collective-permute-start | bytes 5326856 | tf_op jit(solution)/shard_map/ppermute | solution.py:152
  142.3 140.3 %all-gather.10.cloned.1.call-start = ((), (), s32[]{:S(2)}) async-start(), calls=%async_computation.6 | async-start | bytes 2820096 | tf_op jit(solution)/shard_map/all_gather | solution.py:232
  143.0 153.9 %all-gather.12.cloned.1.call-start = ((), (), s32[]{:S(2)}) async-start(), calls=%async_computation.7 | async-start | bytes 2820096 | tf_op jit(solution)/shard_map/all_gather | solution.py:243
  158.9 312.7 %reduce-scatter.12.cloned.1.call-start = ((), (), s32[]{:S(2)}) async-start(), calls=%async_computation.8 | async-start | bytes 7962624 | tf_op jit(solution)/shard_map/reduce_scatter | solution.py:312
  195.1 56.9 %collective-permute-start.5 = (bf16[1088,272]{0,1:T(8,128)(2,1)}, bf16[1088,272]{0,1:T(8,128)(2,1)}, u32[]{:S(2)}, u32[]{:S(2)}) collective-permute-start(bf16[1088,272]{0,1:T(8,128)(2,1)} %copy.198), channel_id=1, source_target_pairs={{0,24},{8,0},{16,8},{24,16},{1,25},{9,1},{17,9},{25,17},{2,26},{10... | collective-permute-start | bytes 1775624 | tf_op jit(solution)/shard_map/ppermute | solution.py:152
  195.1 56.5 %collective-permute-start.4 = (bf16[1088,272]{0,1:T(8,128)(2,1)}, bf16[1088,272]{0,1:T(8,128)(2,1)S(1)}, u32[]{:S(2)}, u32[]{:S(2)}) collective-permute-start(bf16[1088,272]{0,1:T(8,128)(2,1)} %copy.198), channel_id=1, source_target_pairs={{0,16},{8,24},{16,0},{24,8},{1,17},{9,25},{17,1},{25,9},{2,18},{10... | collective-permute-start | bytes 1775624 | tf_op jit(solution)/shard_map/ppermute | solution.py:152
  200.6 50.6 %collective-permute-start.3 = (bf16[1088,272]{0,1:T(8,128)(2,1)}, bf16[1088,272]{0,1:T(8,128)(2,1)S(1)}, u32[]{:S(2)}, u32[]{:S(2)}) collective-permute-start(bf16[1088,272]{0,1:T(8,128)(2,1)} %copy.198), channel_id=1, source_target_pairs={{0,8},{8,16},{16,24},{24,0},{1,9},{9,17},{17,25},{25,1},{2,10},{10... | collective-permute-start | bytes 1775624 | tf_op jit(solution)/shard_map/ppermute | solution.py:152
  272.5 35.3 %collective-permute-start.14 = (bf16[192,1088]{1,0:T(8,128)(2,1)S(1)}, bf16[192,1088]{1,0:T(8,128)(2,1)}, u32[]{:S(2)}, u32[]{:S(2)}) collective-permute-start(bf16[192,1088]{1,0:T(8,128)(2,1)S(1)} %bitcast.286), channel_id=1, source_target_pairs={{0,16},{8,24},{16,0},{24,8},{1,17},{9,25},{17,1},{25,9},{2,18},{10... | collective-permute-start | bytes 1253384 | tf_op jit(solution)/shard_map/ppermute | solution.py:152
  320.2 36.9 %collective-permute-start.18 = (bf16[192,2176]{1,0:T(8,128)(2,1)}, bf16[192,2176]{1,0:T(8,128)(2,1)}, u32[]{:S(2)}, u32[]{:S(2)}) collective-permute-start(bf16[192,2176]{1,0:T(8,128)(2,1)} %get-tuple-element.140), channel_id=1, source_target_pairs={{0,8},{8,16},{16,24},{24,0},{1,9},{9,17},{17,25},{25,1},{2,10},{10... | collective-permute-start | bytes 2506760 | tf_op jit(solution)/shard_map/ppermute | solution.py:162
  320.9 37.6 %collective-permute-start.17 = (bf16[192,2176]{1,0:T(8,128)(2,1)}, bf16[192,2176]{1,0:T(8,128)(2,1)}, u32[]{:S(2)}, u32[]{:S(2)}) collective-permute-start(bf16[192,2176]{1,0:T(8,128)(2,1)} %get-tuple-element.141), channel_id=1, source_target_pairs={{0,16},{8,24},{16,0},{24,8},{1,17},{9,25},{17,1},{25,9},{2,18},{10... | collective-permute-start | bytes 2506760 | tf_op jit(solution)/shard_map/ppermute | solution.py:162
  396.3 177.8 %reduce-scatter.16.cloned.1.call-start = ((), (), s32[]{:S(2)}) async-start(), calls=%async_computation.11 | async-start | bytes 940032
  428.0 147.7 %reduce-scatter.20.cloned.1.call-start = ((), (), s32[]{:S(2)}) async-start(), calls=%async_computation.13 | async-start | bytes 2820096
  434.9 154.7 %reduce-scatter.18.cloned.1.call-start = ((), (), s32[]{:S(2)}) async-start(), calls=%async_computation.12 | async-start | bytes 2820096
  441.7 189.8 %reduce-scatter.14.cloned.1.call-start = ((), (), s32[]{:S(2)}) async-start(), calls=%async_computation.9 | async-start | bytes 2322432 | tf_op jit(solution)/shard_map/reduce_scatter | solution.py:349
  476.3 87.9 %collective-permute-start.19 = (bf16[1088,816]{0,1:T(8,128)(2,1)}, bf16[1088,816]{0,1:T(8,128)(2,1)}, u32[]{:S(2)}, u32[]{:S(2)}) collective-permute-start(bf16[1088,816]{0,1:T(8,128)(2,1)} %convolution_convert_fusion.4), channel_id=1, source_target_pairs={{0,24},{8,0},{16,8},{24,16},{1,25},{9,1},{17,9},{25,17},{2,26},{10... | collective-permute-start | bytes 5326856 | tf_op jit(solution)/shard_map/ppermute | solution.py:162
  480.7 83.5 %collective-permute-start.21 = (bf16[1088,816]{0,1:T(8,128)(2,1)}, bf16[1088,816]{0,1:T(8,128)(2,1)}, u32[]{:S(2)}, u32[]{:S(2)}) collective-permute-start(bf16[1088,816]{0,1:T(8,128)(2,1)} %convolution_convert_fusion.2), channel_id=1, source_target_pairs={{0,8},{8,16},{16,24},{24,0},{1,9},{9,17},{17,25},{25,1},{2,10},{10... | collective-permute-start | bytes 5326856 | tf_op jit(solution)/shard_map/ppermute | solution.py:162
  482.8 81.5 %collective-permute-start.20 = (bf16[1088,816]{0,1:T(8,128)(2,1)}, bf16[1088,816]{0,1:T(8,128)(2,1)}, u32[]{:S(2)}, u32[]{:S(2)}) collective-permute-start(bf16[1088,816]{0,1:T(8,128)(2,1)} %convolution_convert_fusion.3), channel_id=1, source_target_pairs={{0,16},{8,24},{16,0},{24,8},{1,17},{9,25},{17,1},{25,9},{2,18},{10... | collective-permute-start | bytes 5326856 | tf_op jit(solution)/shard_map/ppermute | solution.py:162
  499.8 58.0 %collective-permute-start.22 = (f32[2176]{0:T(1024)S(1)}, f32[2176]{0:T(1024)S(1)}, u32[]{:S(2)}, u32[]{:S(2)}) collective-permute-start(f32[2176]{0:T(1024)S(1)} %get-tuple-element.130), channel_id=1, source_target_pairs={{0,24},{8,0},{16,8},{24,16},{1,25},{9,1},{17,9},{25,17},{2,26},{10... | collective-permute-start | bytes 26120 | tf_op jit(solution)/shard_map/ppermute | solution.py:162
  502.2 57.0 %collective-permute-start.24 = (f32[2176]{0:T(1024)S(1)}, f32[2176]{0:T(1024)S(1)}, u32[]{:S(2)}, u32[]{:S(2)}) collective-permute-start(f32[2176]{0:T(1024)S(1)} %get-tuple-element.131), channel_id=1, source_target_pairs={{0,8},{8,16},{16,24},{24,0},{1,9},{9,17},{17,25},{25,1},{2,10},{10... | collective-permute-start | bytes 26120 | tf_op jit(solution)/shard_map/ppermute | solution.py:162
  577.8 33.3 %collective-permute-start.31 = (bf16[136,272]{1,0:T(8,128)(2,1)S(1)}, bf16[136,272]{1,0:T(8,128)(2,1)S(1)}, u32[]{:S(2)}, u32[]{:S(2)}) collective-permute-start(bf16[136,272]{1,0:T(8,128)(2,1)S(1)} %get-tuple-element.170), channel_id=1, source_target_pairs={{3,0},{7,1},{11,2},{15,3},{19,4},{23,5},{27,6},{31,7},{0,8},{4,9},... | collective-permute-start | bytes 221960 | tf_op jit(solution)/shard_map/ppermute | solution.py:290
  (60 other events, 655.6 us)
Sparse Core Ops, SparseCore 0:
  9.7 30.5 all-gather.7
  142.4 82.0 all-gather.13
  226.2 30.6 all-gather.9
  258.9 32.5 all-gather.11
  396.4 75.2 reduce-scatter.11
  473.8 30.5 reduce-scatter.15
  506.8 36.3 reduce-scatter.19
  545.6 38.0 reduce-scatter.17
  586.1 45.3 reduce-scatter.13

commit v3 on v2

--- a/solution.py
+++ b/solution.py
@@ -9,6 +9,7 @@
 HEAD_DIM = 64
 PAIR = 2 * HEAD_DIM
 PAIRS = (HEADS + 1) // 2
+AT_ONCE = 3
 
 
 EPSILON = 1e-05
@@ -58,49 +59,55 @@
 
 def attend_kernel(first_ref, last_ref, q_ref, kv_ref, out_ref, weights_ref):
     stream = weights_ref.shape[3]
-    keys = kv_ref[:, 0, 0].reshape(stream, PAIR)
-    values = kv_ref[:, 0, 1].reshape(stream, PAIR)
     key_pos = lax.broadcasted_iota(jnp.int32, (q_ref.shape[1], stream), 1)
     visible = (key_pos >= first_ref[0]) & (key_pos <= last_ref[0])
-    attended = []
-    for half in range(2):
-        scores = back_dot(head_part(q_ref[0], half), keys) * SCALE
-        scores = jnp.where(visible, scores, NEGATIVE)
-        weights = jnp.exp(scores - jnp.max(scores, axis=1, keepdims=True))
-        weights = weights / jnp.sum(weights, axis=1, keepdims=True)
-        weights = weights.astype(jnp.bfloat16)
-        weights_ref[0, half] = weights
-        attended.append(dot32(weights, values))
-    out_ref[0] = joined(*attended).astype(jnp.bfloat16)
+    for pair in range(AT_ONCE):
+        lanes = slice(pair * PAIR, (pair + 1) * PAIR)
+        keys = kv_ref[:, 0, 0, :, lanes].reshape(stream, PAIR)
+        values = kv_ref[:, 0, 1, :, lanes].reshape(stream, PAIR)
+        queries = q_ref[0, :, lanes]
+        attended = []
+        for half in range(2):
+            scores = back_dot(head_part(queries, half), keys) * SCALE
+            scores = jnp.where(visible, scores, NEGATIVE)
+            weights = jnp.exp(scores - jnp.max(scores, axis=1, keepdims=True))
+            weights = weights / jnp.sum(weights, axis=1, keepdims=True)
+            weights = weights.astype(jnp.bfloat16)
+            weights_ref[0, 2 * pair + half] = weights
+            attended.append(dot32(weights, values))
+        out_ref[0, :, lanes] = joined(*attended).astype(jnp.bfloat16)
 
 
 def attend_back_kernel(q_ref, kv_ref, grad_ref, weights_ref, grad_q_ref, grad_kv_ref):
     stream = weights_ref.shape[3]
-    keys = kv_ref[:, 0, 0].reshape(stream, PAIR)
-    values = kv_ref[:, 0, 1].reshape(stream, PAIR)
-    grad_q = []
-    grad_k = jnp.zeros((stream, PAIR), jnp.float32)
-    grad_v = jnp.zeros((stream, PAIR), jnp.float32)
-    for half in range(2):
-        weights = weights_ref[0, half]
-        weights32 = weights.astype(jnp.float32)
-        grad = head_part(grad_ref[0], half)
-        grad_weights = back_dot(grad, values)
-        row_dot = jnp.sum(weights32 * grad_weights, axis=1, keepdims=True)
-        grad_scores = (weights32 * (grad_weights - row_dot)).astype(jnp.bfloat16)
-        grad_q.append(dot32(grad_scores, keys))
-        grad_k = grad_k + outer_sum(grad_scores, head_part(q_ref[0], half))
-        grad_v = grad_v + outer_sum(weights, grad)
-    grad_q_ref[0] = (joined(*grad_q) * SCALE).astype(jnp.bfloat16)
     block = grad_kv_ref.shape
-    grad_kv_ref[:, 0, 0] = (grad_k * SCALE).astype(jnp.bfloat16).reshape(block[0], block[3], PAIR)
-    grad_kv_ref[:, 0, 1] = grad_v.astype(jnp.bfloat16).reshape(block[0], block[3], PAIR)
+    shape = (block[0], block[3], PAIR)
+    for pair in range(AT_ONCE):
+        lanes = slice(pair * PAIR, (pair + 1) * PAIR)
+        keys = kv_ref[:, 0, 0, :, lanes].reshape(stream, PAIR)
+        values = kv_ref[:, 0, 1, :, lanes].reshape(stream, PAIR)
+        grad_q = []
+        grad_k = jnp.zeros((stream, PAIR), jnp.float32)
+        grad_v = jnp.zeros((stream, PAIR), jnp.float32)
+        for half in range(2):
+            weights = weights_ref[0, 2 * pair + half]
+            weights32 = weights.astype(jnp.float32)
+            grad = head_part(grad_ref[0, :, lanes], half)
+            grad_weights = back_dot(grad, values)
+            row_dot = jnp.sum(weights32 * grad_weights, axis=1, keepdims=True)
+            grad_scores = (weights32 * (grad_weights - row_dot)).astype(jnp.bfloat16)
+            grad_q.append(dot32(grad_scores, keys))
+            grad_k = grad_k + outer_sum(grad_scores, head_part(q_ref[0, :, lanes], half))
+            grad_v = grad_v + outer_sum(weights, grad)
+        grad_q_ref[0, :, lanes] = (joined(*grad_q) * SCALE).astype(jnp.bfloat16)
+        grad_kv_ref[:, 0, 0, :, lanes] = (grad_k * SCALE).astype(jnp.bfloat16).reshape(shape)
+        grad_kv_ref[:, 0, 1, :, lanes] = grad_v.astype(jnp.bfloat16).reshape(shape)
 
 
 def attention_specs(span, ctx_size):
-    row = pl.BlockSpec((1, span, PAIR), lambda m, p: (m, 0, p))
-    kv = pl.BlockSpec((ctx_size, 1, 2, span, PAIR), lambda m, p: (0, m, 0, 0, p))
-    weights = pl.BlockSpec((1, 2, span, ctx_size * span), lambda m, p: (m, p, 0, 0))
+    row = pl.BlockSpec((1, span, AT_ONCE * PAIR), lambda m, p: (m, 0, p))
+    kv = pl.BlockSpec((ctx_size, 1, 2, span, AT_ONCE * PAIR), lambda m, p: (0, m, 0, 0, p))
+    weights = pl.BlockSpec((1, 2 * AT_ONCE, span, ctx_size * span), lambda m, p: (m, p, 0, 0))
     limit = pl.BlockSpec((1, span, 1), lambda m, p: (m, 0, 0))
     return row, kv, weights, limit
 
@@ -110,7 +117,7 @@
     row, kv, weights, limit = attention_specs(span, ctx_size)
     return pl.pallas_call(
         attend_kernel,
-        grid=(micro, PAIRS),
+        grid=(micro, PAIRS // AT_ONCE),
         in_specs=[limit, limit, row, kv],
         out_specs=[row, weights],
         out_shape=[
@@ -126,7 +133,7 @@
     row, kv, weights, _ = attention_specs(span, ctx_size)
     return pl.pallas_call(
         attend_back_kernel,
-        grid=(micro, PAIRS),
+        grid=(micro, PAIRS // AT_ONCE),
         in_specs=[row, kv, row, weights],
         out_specs=[row, kv],
         out_shape=[
@@ -226,7 +233,13 @@
         vectors.append(small_all[:, start : start + size].reshape(-1).astype(f32))
         start += size
     ln1_scale, ln1_bias, qv_bias, out_bias, ln2_scale, ln2_bias, down_bias = vectors
-    qkv_near = shared(lax.all_gather(w_qkv, "ctx", axis=0, tiled=True))
+    lead = qkv_part // 256 * 128 or qkv_part // 2
+    rest = qkv_part - lead
+    lead_rows = lax.all_gather(w_qkv[:, :lead], "ctx", axis=0, tiled=True)
+    rest_rows = jnp.concatenate(shared(w_qkv[:, lead:]), axis=1)
+    lead_rows, rest_rows = lax.optimization_barrier((lead_rows, rest_rows))
+    rest_near = lax.all_gather(rest_rows, "ctx", axis=0, tiled=True)
+    lead_near = shared(lead_rows)
     out_near = shared(lax.all_gather(w_out, "ctx", axis=0, tiled=True))
     grad_all = jnp.concatenate(shared(grad_out), axis=0)
     up_here = lax.all_gather(w_up, "ctx", axis=0, tiled=True)
@@ -245,7 +258,14 @@
     normed1, normal1, inverse1 = layer_norm(tokens32, ln1_scale, ln1_bias)
     normed1 = normed1.astype(bf16)
     qkv_bias = jnp.concatenate([qv_bias[:width], jnp.zeros((width,), f32), qv_bias[width:]])
-    qkv = swapped([dot32(normed1, piece) for piece in qkv_near], dp_index, -1)
+    rest_qkv = dot32(normed1, rest_near)
+    qkv = [
+        jnp.concatenate(
+            [dot32(normed1, lead_near[k]), rest_qkv[:, k * rest : (k + 1) * rest]], axis=1
+        )
+        for k in range(dp_size)
+    ]
+    qkv = swapped(qkv, dp_index, -1)
     qkv = jnp.concatenate(qkv, axis=1)
     qkv = (qkv + qkv_bias).astype(bf16)
     queries = padded_heads(qkv[:, :width], micro)
@@ -272,18 +292,14 @@
         [dot32(hidden, down_here).astype(bf16), back_dot(grad_upper, up_here).astype(bf16)], axis=1
     )
     both = returned([both[k * rows : (k + 1) * rows] for k in range(dp_size)])
+    up_grad = outer_sum(normed2_all, grad_upper).astype(bf16)
+    down_grad = outer_sum(hidden, grad_all).astype(bf16)
+    both, up_grad, down_grad = lax.optimization_barrier((both, up_grad, down_grad))
     block_out = (residual + both[:, :width] + down_bias).astype(bf16)
     grad_normed2 = both[:, width:]
-    up_grad = lax.psum_scatter(
-        outer_sum(normed2_all, grad_upper).astype(bf16).reshape(ctx_size, -1, up_here.shape[1]),
-        "ctx",
-        scatter_dimension=0,
-    ).astype(f32)
-    down_grad = lax.psum_scatter(
-        outer_sum(hidden, grad_all).astype(bf16).reshape(ctx_size, -1, width),
-        "ctx",
-        scatter_dimension=0,
-    )
+    up_grad = lax.psum_scatter(up_grad.reshape(ctx_size, -1, up_here.shape[1]), "ctx")
+    down_grad = lax.psum_scatter(down_grad.reshape(ctx_size, -1, width), "ctx")
+    kept_down = down_grad
     down_cols = [down_grad[:, j * out_part : (j + 1) * out_part] for j in range(dp_size)]
     down_cols = swapped(down_cols, piece_index, -1)
     down_grad = [
@@ -304,11 +320,16 @@
     for k in range(1, dp_size):
         grad_attended = grad_attended + back_dot(branch_parts[k], out_near[k])
     grad_attended = padded_heads(grad_attended.astype(bf16), micro)
-    out_grads = returned([outer_sum(attended, part).astype(bf16) for part in branch_parts])
-    out_grads = out_grads.astype(bf16)
-    out_grads = out_grads.reshape(ctx_size, -1, out_part)
-    out_grads = lax.psum_scatter(out_grads, "ctx", scatter_dimension=0).astype(f32)
+    out_grads = outer_sum(attended, jnp.concatenate(branch_parts, axis=1)).astype(bf16)
+    out_grads = lax.psum_scatter(out_grads.reshape(ctx_size, -1, width), "ctx")
     grad_queries, grad_kv = attend_back(queries, kv_all, grad_attended, weights)
+    grad_kv, up_grad, kept_down, out_grads = lax.optimization_barrier(
+        (grad_kv, up_grad, kept_down, out_grads)
+    )
+    up_grad = up_grad.astype(f32)
+    out_grads = returned(
+        [out_grads[:, k * out_part : (k + 1) * out_part] for k in range(dp_size)]
+    )
     grad_kv = lax.psum_scatter(grad_kv, "ctx", scatter_dimension=0)
     grad_qkv = jnp.concatenate(
         [
@@ -320,10 +341,15 @@
     )
     pieces = [grad_qkv[:, j * qkv_part : (j + 1) * qkv_part] for j in range(dp_size)]
     pieces = swapped(pieces, dp_index, -1)
-    qkv_grads = returned([outer_sum(normed1, piece).astype(bf16) for piece in pieces])
-    grad_normed1 = back_dot(pieces[0], qkv_near[0])
-    for j in range(1, dp_size):
-        grad_normed1 = grad_normed1 + back_dot(pieces[j], qkv_near[j])
+    lead_pieces = [piece[:, :lead] for piece in pieces]
+    rest_pieces = jnp.concatenate([piece[:, lead:] for piece in pieces], axis=1)
+    rest_grads = outer_sum(normed1, rest_pieces).astype(bf16)
+    rest_grads = lax.psum_scatter(rest_grads.reshape(ctx_size, -1, dp_size * rest), "ctx")
+    rest_grads = returned([rest_grads[:, k * rest : (k + 1) * rest] for k in range(dp_size)])
+    lead_grads = returned([outer_sum(normed1, piece).astype(bf16) for piece in lead_pieces])
+    grad_normed1 = back_dot(rest_pieces, rest_near)
+    for k in range(dp_size):
+        grad_normed1 = grad_normed1 + back_dot(lead_pieces[k], lead_near[k])
     input_grad = (grad_residual + norm_back(grad_normed1, normal1, inverse1, ln1_scale)).astype(
         bf16
     )
@@ -341,14 +367,15 @@
     sums = jnp.concatenate([member.reshape(dp_size, -1) for member in sums], axis=1)
     sums = returned(swapped([sums[j] for j in range(dp_size)], dp_index, -1))
     up_sums = jnp.sum(grad_upper.astype(f32), axis=0)
-    sums = jnp.concatenate([sums, up_sums]).reshape(-1, qkv_part)
-    sums = jnp.pad(sums, ((0, 8 - sums.shape[0]), (0, 0)))
-    sums = jnp.broadcast_to(sums[None], (ctx_size,) + sums.shape)
+    sums = jnp.concatenate([sums, up_sums])
+    sum_rows = -(-sums.shape[0] // (8 * lead)) * 8
+    sums = jnp.pad(sums, (0, sum_rows * lead - sums.shape[0])).reshape(1, sum_rows, lead)
+    sums = jnp.broadcast_to(sums, (ctx_size, sum_rows, lead))
     qkv_rows = width // ctx_size
-    qkv_grads = jnp.concatenate([qkv_grads.reshape(ctx_size, qkv_rows, qkv_part), sums], axis=1)
-    qkv_grads = lax.psum_scatter(qkv_grads.astype(bf16), "ctx", scatter_dimension=0).astype(f32)
-    sums = qkv_grads[qkv_rows:].reshape(-1)
-    qkv_grads = qkv_grads[:qkv_rows]
+    lead_grads = jnp.concatenate([lead_grads.reshape(ctx_size, qkv_rows, lead), sums], axis=1)
+    lead_grads = lax.psum_scatter(lead_grads.astype(bf16), "ctx").astype(f32)
+    sums = lead_grads[qkv_rows:].reshape(-1)
+    qkv_grads = jnp.concatenate([lead_grads[:qkv_rows], rest_grads], axis=1)
     cuts = []
     start = 0
     for member in small + (up_bias,):

time: 653 us -> 721 us (1.10)
  local copies, waits for them, and re-layouts: 53.4 us -> 80.9 us
  starting transfers between devices: 56.6 us -> 76.7 us
  blocking collectives: 44.6 us -> 62.9 us
  other arithmetic: 26.6 us -> 40.6 us
  waiting for transfers between devices: 328 us -> 320 us
  Pallas kernels: 48.8 us -> 41.4 us
    unnamed x12 -> x14, waiting for transfers between devices: 1.52 us -> 72 us
    ppermute x12 -> x15, waiting for transfers between devices: 121 us -> 54 us  [returned(): total = total + lax.ppermute(blocks[k], 'dp', route).astype(jnp.float32)]
    ppermute x12 -> x15, waiting for transfers between devices: 97.6 us -> 49.1 us  [shared(): lax.ppermute(block, 'dp', [(s, (s + k) % count) for s in range(count)])]
    reduce_scatter x1, waiting for transfers between devices: 29.4 us -> 77 us  [local(): grad_kv = lax.psum_scatter(grad_kv, 'ctx', scatter_dimension=0)]
    reduce_scatter x1, waiting for transfers between devices: 13.6 us -> 40.5 us  [local(): lax.psum_scatter(rest_grads.reshape(ctx_size, -1, dp_size * rest), 'ctx')]
    all_gather x1, waiting for transfers between devices: 16.5 us -> 0.02 us  [local(): rest_near = lax.all_gather(rest_rows, 'ctx', axis=0, tiled=True)]
    all_gather x0 -> x1, blocking collectives: none -> 16.1 us  [local(): lead_rows = lax.all_gather(w_qkv[:, :lead], 'ctx', axis=0, tiled=True)]
    ppermute x12 -> x15, starting transfers between devices: 19.4 us -> 32.6 us  [shared(): lax.ppermute(block, 'dp', [(s, (s + k) % count) for s in range(count)])]
  transfers between devices with their start and end apart: 41 -> 48, of which waited for: 21 -> 19; matrix products, arithmetic and copies ran while one was open for 16% -> 16% of each run, Pallas kernels for 4% -> 6%
where the time goes in v3:
time: 721 us; the launch traced here: 712 us
  waiting for transfers between devices  320 us (44%)
  local copies, waits for them, and re-layouts  80.9 us (11%)
  starting transfers between devices  76.7 us (11%)
  matrix products  74.1 us (10%)
  blocking collectives  62.9 us (9%)
  Pallas kernels  41.4 us (6%)
  other arithmetic  40.6 us (6%)
  between operations  15.8 us (2%)
    reduce_scatter x1, waiting for transfers between devices, local(): grad_kv = lax.psum_scatter(grad_kv, 'ctx', scatter_dimension=0)  77 us
    unnamed x14, waiting for transfers between devices  72 us
    ppermute x15, waiting for transfers between devices, returned(): total = total + lax.ppermute(blocks[k], 'dp', route).astype(jnp.float32)  54 us
    ppermute x15, waiting for transfers between devices, shared(): lax.ppermute(block, 'dp', [(s, (s + k) % count) for s in range(count)])  49.1 us
    reduce_scatter x1, waiting for transfers between devices, local(): lax.psum_scatter(rest_grads.reshape(ctx_size, -1, dp_size * rest), 'ctx')  40.5 us
    all_gather x1, blocking collectives, local(): out_near = shared(lax.all_gather(w_out, 'ctx', axis=0, tiled=True))  37.8 us
    ppermute x15, starting transfers between devices, shared(): lax.ppermute(block, 'dp', [(s, (s + k) % count) for s in range(count)])  32.6 us
    dot_general x11, matrix products, dot32(): return jnp.dot(left, right, preferred_element_type=jnp.float32)  26.8 us
  transfers between devices with their start and end apart: 48, of which 19 were waited for; matrix products, arithmetic and copies ran while one was open for 16% of the time, Pallas kernels for 6%

profile of v3, /device:TPU:0, one launch (start us, length us, event | category | flops | bytes accessed | tf_op | source)
XLA Modules:
  0.0 712.0 jit_solution(12064282486774293735)
XLA Ops:
  14.2 16.1 %all_gather.29 = bf16[1088,384]{1,0:T(8,128)(2,1)S(1)} all-gather(bf16[136,384]{1,0:T(8,128)(2,1)S(1)} %slice.246), channel_id=1, replica_groups=mesh['dp'=4,'ctx'=8] {'ctx'}, dimensions={0}, use_global_device_ids=true | all-gather | bytes 940032 | tf_op jit(solution)/shard_map/all_gather | solution.py:238
  32.2 9.1 %all-gather.2 = bf16[4,1,2176]{2,1,0:T(2,128)(2,1)S(1)} all-gather(bf16[1,1,2176]{2,1,0:T(2,128)(2,1)S(1)} %reshape.322), channel_id=2, replica_groups=mesh['dp'=4,'ctx'=8] {'dp'}, dimensions={0}, use_global_device_ids=true | all-gather | bytes 21760 | tf_op jit(solution)/shard_map/all_gather | solution.py:228
  47.1 17.1 %collective-permute-done.5 = bf16[1088,384]{1,0:T(8,128)(2,1)S(1)} collective-permute-done((bf16[1088,384]{1,0:T(8,128)(2,1)S(1)}, bf16[1088,384]{1,0:T(8,128)(2,1)S(1)}, u32[]{:S(2)}, u32[]{:S(2)}) %collective-permute-start.5) | collective-permute-done | bytes 835616 | tf_op jit(solution)/shard_map/ppermute | solution.py:159
  65.3 15.8 %collective-permute-done.4 = bf16[1088,384]{1,0:T(8,128)(2,1)} collective-permute-done((bf16[1088,384]{1,0:T(8,128)(2,1)S(1)}, bf16[1088,384]{1,0:T(8,128)(2,1)}, u32[]{:S(2)}, u32[]{:S(2)}) %collective-permute-start.4) | collective-permute-done | bytes 835616 | tf_op jit(solution)/shard_map/ppermute | solution.py:159
  106.0 6.3 collective-permute-start.13
  114.7 37.8 %all_gather.33 = bf16[1088,272]{1,0:T(8,128)(2,1)S(1)} all-gather(bf16[136,272]{1,0:T(8,128)(2,1)S(1)} %copy-done.34), channel_id=1, replica_groups=mesh['dp'=4,'ctx'=8] {'ctx'}, dimensions={0}, use_global_device_ids=true | all-gather | bytes 665856 | tf_op jit(solution)/shard_map/all_gather | solution.py:243
  157.8 13.5 %collective-permute-start.6 = (bf16[1088,272]{0,1:T(8,128)(2,1)}, bf16[1088,272]{0,1:T(8,128)(2,1)}, u32[]{:S(2)}, u32[]{:S(2)}) collective-permute-start(bf16[1088,272]{0,1:T(8,128)(2,1)} %copy.148), channel_id=1, source_target_pairs={{0,8},{8,16},{16,24},{24,0},{1,9},{9,17},{17,25},{25,1},{2,10},{10... | collective-permute-start | bytes 1775624 | tf_op jit(solution)/shard_map/ppermute | solution.py:159
  173.0 10.1 %all-gather.14.cloned.1.call-done = bf16[24,2,64,1152]{3,2,1,0:T(8,128)(2,1)} async-done(((bf16[3,2,64,1152]{3,2,1,0:T(8,128)(2,1)}), bf16[24,2,64,1152]{3,2,1,0:T(8,128)(2,1)}) %all-gather.14.cloned.1.call-update) | async-done | bytes 7077904 | tf_op jit(solution)/shard_map/all_gather | solution.py:274
  186.2 20.3 %shard_map.254 = (bf16[3,64,1152]{2,1,0:T(8,128)(2,1)S(1)}, bf16[3,18,64,512]{3,2,1,0:T(8,128)(2,1)S(1)}) custom-call(s32[3,64,1]{2,1,0:T(8,128)S(1)} %copy.147.first_ref, s32[3,64,1]{2,1,0:T(8,128)S(1)} %broadcast_in_dim.22.last_ref, bf16[3,64,1152]{2,1,0:T(8,128)(2,1)S(1)} %bitcast.201, bf16[8,3,2,64,1152]{4,3,2,1,0:T(8,128)(2,1)S(1)} %bitcast.199), custom_call_target="tpu_custom_call" | custom-call | tf_op jit(solution)/shard_map/pallas_call | solution.py:118
  236.8 7.4 %collective-permute-done.11 = bf16[192,1088]{1,0:T(8,128)(2,1)} collective-permute-done((bf16[192,1088]{1,0:T(8,128)(2,1)}, bf16[192,1088]{1,0:T(8,128)(2,1)}, u32[]{:S(2)}, u32[]{:S(2)}) %collective-permute-start.11) | collective-permute-done | bytes 417824 | tf_op jit(solution)/shard_map/ppermute | solution.py:159
  247.5 7.2 %collective-permute-done.10 = bf16[192,1088]{1,0:T(8,128)(2,1)} collective-permute-done((bf16[192,1088]{1,0:T(8,128)(2,1)}, bf16[192,1088]{1,0:T(8,128)(2,1)}, u32[]{:S(2)}, u32[]{:S(2)}) %collective-permute-start.10) | collective-permute-done | bytes 417824 | tf_op jit(solution)/shard_map/ppermute | solution.py:159
  258.8 6.6 convolution_add_fusion
  272.7 5.8 convert_reduce_fusion
  294.8 6.0 convolution_convert_fusion.3
  300.8 5.7 convolution_convert_fusion.2
  306.5 21.9 %collective-permute-done.20 = bf16[192,2176]{1,0:T(8,128)(2,1)} collective-permute-done((bf16[192,2176]{1,0:T(8,128)(2,1)}, bf16[192,2176]{1,0:T(8,128)(2,1)}, u32[]{:S(2)}, u32[]{:S(2)}) %collective-permute-start.20) | collective-permute-done | bytes 835616 | tf_op jit(solution)/shard_map/ppermute | solution.py:169
  360.6 21.1 %shard_map.255 = (bf16[3,64,1152]{2,1,0:T(8,128)(2,1)S(1)}, bf16[8,3,2,64,1152]{4,3,2,1,0:T(8,128)(2,1)S(1)}) custom-call(bf16[3,64,1152]{2,1,0:T(8,128)(2,1)S(1)} %bitcast.202, bf16[8,3,2,64,1152]{4,3,2,1,0:T(8,128)(2,1)S(1)} %bitcast.200, bf16[3,64,1152]{2,1,0:T(8,128)(2,1)S(1)} %bitcast.206, bf16[3,18,64,512]{3,2,1,0:T(8,128)(2,1)S(1)} %copy-done.4), custom_call_target="tpu_custom_call" | custom-call | tf_op jit(solution)/shard_map/pallas_call | solution.py:134
  384.5 30.9 %reduce-scatter.19.cloned.1.call-done = bf16[1,136,1088]{2,1,0:T(8,128)(2,1)} async-done(((bf16[8,136,1088]{2,1,0:T(8,128)(2,1)}), bf16[1,136,1088]{2,1,0:T(8,128)(2,1)}) %reduce-scatter.19.cloned.1.call-update) | async-done | bytes 295952
  415.4 39.7 %reduce-scatter.23.cloned.1.call-done = bf16[1,136,1088]{2,1,0:T(8,128)(2,1)} async-done(((bf16[8,136,1088]{2,1,0:T(8,128)(2,1)}), bf16[1,136,1088]{2,1,0:T(8,128)(2,1)}) %reduce-scatter.23.cloned.1.call-update) | async-done | bytes 295952
  456.6 77.0 %reduce-scatter.15.cloned.1.call-done = bf16[1,3,2,64,1152]{4,3,2,1,0:T(8,128)(2,1)} async-done(((bf16[8,3,2,64,1152]{4,3,2,1,0:T(8,128)(2,1)}), bf16[1,3,2,64,1152]{4,3,2,1,0:T(8,128)(2,1)}) %reduce-scatter.15.cloned.1.call-update) | async-done | bytes 884752 | tf_op jit(solution)/shard_map/reduce_scatter | solution.py:333
  566.7 24.2 %collective-permute-done.25 = f32[2176]{0:T(1024)S(1)} collective-permute-done((f32[2176]{0:T(1024)S(1)}, f32[2176]{0:T(1024)S(1)}, u32[]{:S(2)}, u32[]{:S(2)}) %collective-permute-start.25) | collective-permute-done | bytes 8736 | tf_op jit(solution)/shard_map/ppermute | solution.py:169
  603.1 6.3 collective-permute-start.37
  620.8 13.4 %collective-permute-done.37 = bf16[136,272]{1,0:T(8,128)(2,1)S(1)} collective-permute-done((bf16[136,272]{1,0:T(8,128)(2,1)S(1)}, bf16[136,272]{1,0:T(8,128)(2,1)S(1)}, u32[]{:S(2)}, u32[]{:S(2)}) %collective-permute-start.37) | collective-permute-done | bytes 74016 | tf_op jit(solution)/shard_map/ppermute | solution.py:306
  652.3 40.5 %reduce-scatter.17.cloned.1.call-done = bf16[1,136,1728]{2,1,0:T(8,128)(2,1)} async-done(((bf16[8,136,1728]{2,1,0:T(8,128)(2,1)}), bf16[1,136,1728]{2,1,0:T(8,128)(2,1)}) %reduce-scatter.17.cloned.1.call-update) | async-done | bytes 470032 | tf_op jit(solution)/shard_map/reduce_scatter | solution.py:347
  (388 shorter events, 236.4 us)
Async XLA Ops:
  7.2 77.8 %all-gather.8.cloned.1.call-start = ((), (), s32[]{:S(2)}) async-start(), calls=%async_computation.6 | async-start | bytes 4386816 | tf_op jit(solution)/shard_map/all_gather | solution.py:241
  31.4 151.7 %all-gather.14.cloned.1.call-start = ((), (), s32[]{:S(2)}) async-start(), calls=%async_computation.11 | async-start | bytes 7962624 | tf_op jit(solution)/shard_map/all_gather | solution.py:274
  44.5 36.6 %collective-permute-start.4 = (bf16[1088,384]{1,0:T(8,128)(2,1)S(1)}, bf16[1088,384]{1,0:T(8,128)(2,1)}, u32[]{:S(2)}, u32[]{:S(2)}) collective-permute-start(bf16[1088,384]{1,0:T(8,128)(2,1)S(1)} %all_gather.29), channel_id=1, source_target_pairs={{0,16},{8,24},{16,0},{24,8},{1,17},{9,25},{17,1},{25,9},{2,18},{10... | collective-permute-start | bytes 2506760 | tf_op jit(solution)/shard_map/ppermute | solution.py:159
  45.1 38.3 %collective-permute-start.3 = (bf16[1088,384]{1,0:T(8,128)(2,1)S(1)}, bf16[1088,384]{1,0:T(8,128)(2,1)}, u32[]{:S(2)}, u32[]{:S(2)}) collective-permute-start(bf16[1088,384]{1,0:T(8,128)(2,1)S(1)} %all_gather.29), channel_id=1, source_target_pairs={{0,8},{8,16},{16,24},{24,0},{1,9},{9,17},{17,25},{25,1},{2,10},{10... | collective-permute-start | bytes 2506760 | tf_op jit(solution)/shard_map/ppermute | solution.py:159
  99.2 159.6 %all-gather.10.cloned.1.call-start = ((), (), s32[]{:S(2)}) async-start(), calls=%async_computation.7 | async-start | bytes 2820096 | tf_op jit(solution)/shard_map/all_gather | solution.py:245
  100.0 165.5 %all-gather.12.cloned.1.call-start = ((), (), s32[]{:S(2)}) async-start(), calls=%async_computation.8 | async-start | bytes 2820096 | tf_op jit(solution)/shard_map/all_gather | solution.py:256
  114.6 269.9 %reduce-scatter.21.cloned.1.call-start = ((), (), s32[]{:S(2)}) async-start(), calls=%async_computation.13 | async-start | bytes 2820096
  153.6 56.3 %collective-permute-start.8 = (bf16[1088,272]{0,1:T(8,128)(2,1)}, bf16[1088,272]{0,1:T(8,128)(2,1)}, u32[]{:S(2)}, u32[]{:S(2)}) collective-permute-start(bf16[1088,272]{0,1:T(8,128)(2,1)} %copy.148), channel_id=1, source_target_pairs={{0,24},{8,0},{16,8},{24,16},{1,25},{9,1},{17,9},{25,17},{2,26},{10... | collective-permute-start | bytes 1775624 | tf_op jit(solution)/shard_map/ppermute | solution.py:159
  153.6 54.9 %collective-permute-start.7 = (bf16[1088,272]{0,1:T(8,128)(2,1)}, bf16[1088,272]{0,1:T(8,128)(2,1)}, u32[]{:S(2)}, u32[]{:S(2)}) collective-permute-start(bf16[1088,272]{0,1:T(8,128)(2,1)} %copy.148), channel_id=1, source_target_pairs={{0,16},{8,24},{16,0},{24,8},{1,17},{9,25},{17,1},{25,9},{2,18},{10... | collective-permute-start | bytes 1775624 | tf_op jit(solution)/shard_map/ppermute | solution.py:159
  157.8 48.7 %collective-permute-start.6 = (bf16[1088,272]{0,1:T(8,128)(2,1)}, bf16[1088,272]{0,1:T(8,128)(2,1)}, u32[]{:S(2)}, u32[]{:S(2)}) collective-permute-start(bf16[1088,272]{0,1:T(8,128)(2,1)} %copy.148), channel_id=1, source_target_pairs={{0,8},{8,16},{16,24},{24,0},{1,9},{9,17},{17,25},{25,1},{2,10},{10... | collective-permute-start | bytes 1775624 | tf_op jit(solution)/shard_map/ppermute | solution.py:159
  233.4 37.6 %collective-permute-start.18 = (bf16[192,1088]{1,0:T(8,128)(2,1)}, bf16[192,1088]{1,0:T(8,128)(2,1)}, u32[]{:S(2)}, u32[]{:S(2)}) collective-permute-start(bf16[192,1088]{1,0:T(8,128)(2,1)} %bitcast.229), channel_id=1, source_target_pairs={{0,24},{8,0},{16,8},{24,16},{1,25},{9,1},{17,9},{25,17},{2,26},{10... | collective-permute-start | bytes 1253384 | tf_op jit(solution)/shard_map/ppermute | solution.py:159
  235.6 37.1 %collective-permute-start.17 = (bf16[192,1088]{1,0:T(8,128)(2,1)}, bf16[192,1088]{1,0:T(8,128)(2,1)}, u32[]{:S(2)}, u32[]{:S(2)}) collective-permute-start(bf16[192,1088]{1,0:T(8,128)(2,1)} %bitcast.230), channel_id=1, source_target_pairs={{0,16},{8,24},{16,0},{24,8},{1,17},{9,25},{17,1},{25,9},{2,18},{10... | collective-permute-start | bytes 1253384 | tf_op jit(solution)/shard_map/ppermute | solution.py:159
  291.1 37.4 %collective-permute-start.20 = (bf16[192,2176]{1,0:T(8,128)(2,1)}, bf16[192,2176]{1,0:T(8,128)(2,1)}, u32[]{:S(2)}, u32[]{:S(2)}) collective-permute-start(bf16[192,2176]{1,0:T(8,128)(2,1)} %copy.165), channel_id=1, source_target_pairs={{0,16},{8,24},{16,0},{24,8},{1,17},{9,25},{17,1},{25,9},{2,18},{10... | collective-permute-start | bytes 2506760 | tf_op jit(solution)/shard_map/ppermute | solution.py:169
  291.9 38.9 %collective-permute-start.21 = (bf16[192,2176]{1,0:T(8,128)(2,1)}, bf16[192,2176]{1,0:T(8,128)(2,1)}, u32[]{:S(2)}, u32[]{:S(2)}) collective-permute-start(bf16[192,2176]{1,0:T(8,128)(2,1)} %copy.167), channel_id=1, source_target_pairs={{0,8},{8,16},{16,24},{24,0},{1,9},{9,17},{17,25},{25,1},{2,10},{10... | collective-permute-start | bytes 2506760 | tf_op jit(solution)/shard_map/ppermute | solution.py:169
  292.5 40.5 %collective-permute-start.19 = (bf16[192,2176]{1,0:T(8,128)(2,1)}, bf16[192,2176]{1,0:T(8,128)(2,1)}, u32[]{:S(2)}, u32[]{:S(2)}) collective-permute-start(bf16[192,2176]{1,0:T(8,128)(2,1)} %copy.163), channel_id=1, source_target_pairs={{0,24},{8,0},{16,8},{24,16},{1,25},{9,1},{17,9},{25,17},{2,26},{10... | collective-permute-start | bytes 2506760 | tf_op jit(solution)/shard_map/ppermute | solution.py:169
  339.6 75.9 %reduce-scatter.19.cloned.1.call-start = ((), (), s32[]{:S(2)}) async-start(), calls=%async_computation.12 | async-start | bytes 2820096
  340.2 115.0 %reduce-scatter.23.cloned.1.call-start = ((), (), s32[]{:S(2)}) async-start(), calls=%async_computation.14 | async-start | bytes 2820096
  350.9 182.8 %reduce-scatter.15.cloned.1.call-start = ((), (), s32[]{:S(2)}) async-start(), calls=%async_computation.9 | async-start | bytes 7962624 | tf_op jit(solution)/shard_map/reduce_scatter | solution.py:333
  455.2 194.2 %reduce-scatter.25.cloned.1.call-start = ((), (), s32[]{:S(2)}) async-start(), calls=%async_computation.15 | async-start | bytes 1050624
  553.2 41.4 %collective-permute-start.24 = (bf16[1088,384]{1,0:T(8,128)(2,1)}, bf16[1088,384]{1,0:T(8,128)(2,1)}, u32[]{:S(2)}, u32[]{:S(2)}) collective-permute-start(bf16[1088,384]{1,0:T(8,128)(2,1)} %convolution_convert_fusion.6), channel_id=1, source_target_pairs={{0,8},{8,16},{16,24},{24,0},{1,9},{9,17},{17,25},{25,1},{2,10},{10... | collective-permute-start | bytes 2506760 | tf_op jit(solution)/shard_map/ppermute | solution.py:169
  554.7 39.9 %collective-permute-start.23 = (bf16[1088,384]{1,0:T(8,128)(2,1)}, bf16[1088,384]{1,0:T(8,128)(2,1)}, u32[]{:S(2)}, u32[]{:S(2)}) collective-permute-start(bf16[1088,384]{1,0:T(8,128)(2,1)} %convolution_convert_fusion.7), channel_id=1, source_target_pairs={{0,16},{8,24},{16,0},{24,8},{1,17},{9,25},{17,1},{25,9},{2,18},{10... | collective-permute-start | bytes 2506760 | tf_op jit(solution)/shard_map/ppermute | solution.py:169
  556.2 38.5 %collective-permute-start.22 = (bf16[1088,384]{1,0:T(8,128)(2,1)}, bf16[1088,384]{1,0:T(8,128)(2,1)}, u32[]{:S(2)}, u32[]{:S(2)}) collective-permute-start(bf16[1088,384]{1,0:T(8,128)(2,1)} %convolution_convert_fusion.8), channel_id=1, source_target_pairs={{0,24},{8,0},{16,8},{24,16},{1,25},{9,1},{17,9},{25,17},{2,26},{10... | collective-permute-start | bytes 2506760 | tf_op jit(solution)/shard_map/ppermute | solution.py:169
  597.9 94.9 %reduce-scatter.17.cloned.1.call-start = ((), (), s32[]{:S(2)}) async-start(), calls=%async_computation.10 | async-start | bytes 4386816 | tf_op jit(solution)/shard_map/reduce_scatter | solution.py:347
  603.1 31.0 %collective-permute-start.37 = (bf16[136,272]{1,0:T(8,128)(2,1)S(1)}, bf16[136,272]{1,0:T(8,128)(2,1)S(1)}, u32[]{:S(2)}, u32[]{:S(2)}) collective-permute-start(bf16[136,272]{1,0:T(8,128)(2,1)S(1)} %get-tuple-element.181), channel_id=1, source_target_pairs={{3,0},{7,1},{11,2},{15,3},{19,4},{23,5},{27,6},{31,7},{0,8},{4,9},... | collective-permute-start | bytes 221960 | tf_op jit(solution)/shard_map/ppermute | solution.py:306
  (87 other events, 1219.8 us)
Sparse Core Ops, SparseCore 0:
  31.5 45.7 all-gather.7
  99.3 83.7 all-gather.13
  184.8 30.0 all-gather.9
  216.9 32.4 all-gather.11
  339.7 36.0 reduce-scatter.20
  378.1 37.3 reduce-scatter.18
  417.8 37.3 reduce-scatter.22
  457.6 76.0 reduce-scatter.14
  598.1 44.2 reduce-scatter.24
  644.6 48.2 reduce-scatter.16

commit v4 on v3

--- a/solution.py
+++ b/solution.py
@@ -294,12 +294,11 @@
     both = returned([both[k * rows : (k + 1) * rows] for k in range(dp_size)])
     up_grad = outer_sum(normed2_all, grad_upper).astype(bf16)
     down_grad = outer_sum(hidden, grad_all).astype(bf16)
-    both, up_grad, down_grad = lax.optimization_barrier((both, up_grad, down_grad))
+    both, up_grad = lax.optimization_barrier((both, up_grad))
     block_out = (residual + both[:, :width] + down_bias).astype(bf16)
     grad_normed2 = both[:, width:]
     up_grad = lax.psum_scatter(up_grad.reshape(ctx_size, -1, up_here.shape[1]), "ctx")
     down_grad = lax.psum_scatter(down_grad.reshape(ctx_size, -1, width), "ctx")
-    kept_down = down_grad
     down_cols = [down_grad[:, j * out_part : (j + 1) * out_part] for j in range(dp_size)]
     down_cols = swapped(down_cols, piece_index, -1)
     down_grad = [
@@ -320,16 +319,12 @@
     for k in range(1, dp_size):
         grad_attended = grad_attended + back_dot(branch_parts[k], out_near[k])
     grad_attended = padded_heads(grad_attended.astype(bf16), micro)
-    out_grads = outer_sum(attended, jnp.concatenate(branch_parts, axis=1)).astype(bf16)
-    out_grads = lax.psum_scatter(out_grads.reshape(ctx_size, -1, width), "ctx")
+    out_grads = returned([outer_sum(attended, part).astype(bf16) for part in branch_parts])
+    out_grads = out_grads.astype(bf16).reshape(ctx_size, -1, out_part)
+    out_grads = lax.psum_scatter(out_grads, "ctx").astype(f32)
     grad_queries, grad_kv = attend_back(queries, kv_all, grad_attended, weights)
-    grad_kv, up_grad, kept_down, out_grads = lax.optimization_barrier(
-        (grad_kv, up_grad, kept_down, out_grads)
-    )
+    grad_kv, up_grad = lax.optimization_barrier((grad_kv, up_grad))
     up_grad = up_grad.astype(f32)
-    out_grads = returned(
-        [out_grads[:, k * out_part : (k + 1) * out_part] for k in range(dp_size)]
-    )
     grad_kv = lax.psum_scatter(grad_kv, "ctx", scatter_dimension=0)
     grad_qkv = jnp.concatenate(
         [
@@ -343,10 +338,7 @@
     pieces = swapped(pieces, dp_index, -1)
     lead_pieces = [piece[:, :lead] for piece in pieces]
     rest_pieces = jnp.concatenate([piece[:, lead:] for piece in pieces], axis=1)
-    rest_grads = outer_sum(normed1, rest_pieces).astype(bf16)
-    rest_grads = lax.psum_scatter(rest_grads.reshape(ctx_size, -1, dp_size * rest), "ctx")
-    rest_grads = returned([rest_grads[:, k * rest : (k + 1) * rest] for k in range(dp_size)])
-    lead_grads = returned([outer_sum(normed1, piece).astype(bf16) for piece in lead_pieces])
+    qkv_grads = returned([outer_sum(normed1, piece).astype(bf16) for piece in pieces])
     grad_normed1 = back_dot(rest_pieces, rest_near)
     for k in range(dp_size):
         grad_normed1 = grad_normed1 + back_dot(lead_pieces[k], lead_near[k])
@@ -367,15 +359,14 @@
     sums = jnp.concatenate([member.reshape(dp_size, -1) for member in sums], axis=1)
     sums = returned(swapped([sums[j] for j in range(dp_size)], dp_index, -1))
     up_sums = jnp.sum(grad_upper.astype(f32), axis=0)
-    sums = jnp.concatenate([sums, up_sums])
-    sum_rows = -(-sums.shape[0] // (8 * lead)) * 8
-    sums = jnp.pad(sums, (0, sum_rows * lead - sums.shape[0])).reshape(1, sum_rows, lead)
-    sums = jnp.broadcast_to(sums, (ctx_size, sum_rows, lead))
+    sums = jnp.concatenate([sums, up_sums]).reshape(-1, qkv_part)
+    sums = jnp.pad(sums, ((0, 8 - sums.shape[0]), (0, 0)))
+    sums = jnp.broadcast_to(sums[None], (ctx_size,) + sums.shape)
     qkv_rows = width // ctx_size
-    lead_grads = jnp.concatenate([lead_grads.reshape(ctx_size, qkv_rows, lead), sums], axis=1)
-    lead_grads = lax.psum_scatter(lead_grads.astype(bf16), "ctx").astype(f32)
-    sums = lead_grads[qkv_rows:].reshape(-1)
-    qkv_grads = jnp.concatenate([lead_grads[:qkv_rows], rest_grads], axis=1)
+    qkv_grads = jnp.concatenate([qkv_grads.reshape(ctx_size, qkv_rows, qkv_part), sums], axis=1)
+    qkv_grads = lax.psum_scatter(qkv_grads.astype(bf16), "ctx").astype(f32)
+    sums = qkv_grads[qkv_rows:].reshape(-1)
+    qkv_grads = qkv_grads[:qkv_rows]
     cuts = []
     start = 0
     for member in small + (up_bias,):

time: 721 us -> 631 us (0.88)
  waiting for transfers between devices: 320 us -> 225 us
  matrix products: 74.1 us -> 82.6 us
  local copies, waits for them, and re-layouts: 80.9 us -> 88.4 us
    unnamed x14 -> x12, waiting for transfers between devices: 72 us -> 0.84 us
    ppermute x15 -> x12, waiting for transfers between devices: 54 us -> 101 us  [returned(): total = total + lax.ppermute(blocks[k], 'dp', route).astype(jnp.float32)]
    reduce_scatter x1, waiting for transfers between devices: 77 us -> 33.1 us  [local(): grad_kv = lax.psum_scatter(grad_kv, 'ctx', scatter_dimension=0)]
    reduce_scatter x1, waiting for transfers between devices: 40.5 us -> 0.01 us  [local(): qkv_grads = lax.psum_scatter(qkv_grads.astype(bf16), 'ctx').astype(f32)]
    ppermute x4, waiting for transfers between devices: 15.9 us -> 27.9 us  [local(): lax.ppermute(down_cols[k], ('dp', 'ctx'), [(b, a) for a, b in piece_route...]
    dot_general x8 -> x10, matrix products: 23.6 us -> 30.1 us  [outer_sum(): lax.dot_general(left, right, (((0,), (0,)), ((), ())), preferred_element_...]
    ppermute x15 -> x12, starting transfers between devices: 20.5 us -> 16 us  [returned(): total = total + lax.ppermute(blocks[k], 'dp', route).astype(jnp.float32)]
    unnamed x131 -> x143, local copies, waits for them, and re-layouts: 16.2 us -> 12.9 us
  transfers between devices with their start and end apart: 48 -> 44, of which waited for: 19 -> 18; matrix products, arithmetic and copies ran while one was open for 16% -> 26% of each run, Pallas kernels for 6% -> 7%
where the time goes in v4:
time: 631 us; the launch traced here: 622 us
  waiting for transfers between devices  225 us (36%)
  local copies, waits for them, and re-layouts  88.4 us (14%)
  matrix products  82.6 us (13%)
  starting transfers between devices  73 us (12%)
  blocking collectives  57.6 us (9%)
  Pallas kernels  41.4 us (7%)
  other arithmetic  38.3 us (6%)
  between operations  15.5 us (2%)
    ppermute x12, waiting for transfers between devices, returned(): total = total + lax.ppermute(blocks[k], 'dp', route).astype(jnp.float32)  101 us
    ppermute x15, waiting for transfers between devices, shared(): lax.ppermute(block, 'dp', [(s, (s + k) % count) for s in range(count)])  46.3 us
    all_gather x1, blocking collectives, local(): out_near = shared(lax.all_gather(w_out, 'ctx', axis=0, tiled=True))  34.4 us
    reduce_scatter x1, waiting for transfers between devices, local(): grad_kv = lax.psum_scatter(grad_kv, 'ctx', scatter_dimension=0)  33.1 us
    ppermute x15, starting transfers between devices, shared(): lax.ppermute(block, 'dp', [(s, (s + k) % count) for s in range(count)])  32.7 us
    dot_general x10, matrix products, outer_sum(): lax.dot_general(left, right, (((0,), (0,)), ((), ())), preferred_element_...  30.1 us
    ppermute x4, waiting for transfers between devices, local(): lax.ppermute(down_cols[k], ('dp', 'ctx'), [(b, a) for a, b in piece_route...  27.9 us
    dot_general x11, matrix products, dot32(): return jnp.dot(left, right, preferred_element_type=jnp.float32)  27.4 us
  transfers between devices with their start and end apart: 44, of which 18 were waited for; matrix products, arithmetic and copies ran while one was open for 26% of the time, Pallas kernels for 7%

profile of v4, /device:TPU:0, one launch (start us, length us, event | category | flops | bytes accessed | tf_op | source)
XLA Modules:
  0.0 621.5 jit_solution(1468981473442347682)
XLA Ops:
  15.2 15.9 %all_gather.29 = bf16[1088,384]{1,0:T(8,128)(2,1)S(1)} all-gather(bf16[136,384]{1,0:T(8,128)(2,1)S(1)} %slice.222), channel_id=1, replica_groups=mesh['dp'=4,'ctx'=8] {'ctx'}, dimensions={0}, use_global_device_ids=true | all-gather | bytes 940032 | tf_op jit(solution)/shard_map/all_gather | solution.py:238
  32.4 7.3 %all-gather.2 = bf16[4,1,2176]{2,1,0:T(2,128)(2,1)S(1)} all-gather(bf16[1,1,2176]{2,1,0:T(2,128)(2,1)S(1)} %reshape.423), channel_id=2, replica_groups=mesh['dp'=4,'ctx'=8] {'dp'}, dimensions={0}, use_global_device_ids=true | all-gather | bytes 21760 | tf_op jit(solution)/shard_map/all_gather | solution.py:228
  49.3 17.0 %collective-permute-done.3 = bf16[1088,384]{1,0:T(8,128)(2,1)} collective-permute-done((bf16[1088,384]{1,0:T(8,128)(2,1)S(1)}, bf16[1088,384]{1,0:T(8,128)(2,1)}, u32[]{:S(2)}, u32[]{:S(2)}) %collective-permute-start.3) | collective-permute-done | bytes 835616 | tf_op jit(solution)/shard_map/ppermute | solution.py:159
  68.6 12.9 %collective-permute-done.4 = bf16[1088,384]{1,0:T(8,128)(2,1)} collective-permute-done((bf16[1088,384]{1,0:T(8,128)(2,1)S(1)}, bf16[1088,384]{1,0:T(8,128)(2,1)}, u32[]{:S(2)}, u32[]{:S(2)}) %collective-permute-start.4) | collective-permute-done | bytes 835616 | tf_op jit(solution)/shard_map/ppermute | solution.py:159
  119.0 34.4 %all_gather.33 = bf16[1088,272]{1,0:T(8,128)(2,1)S(1)} all-gather(bf16[136,272]{1,0:T(8,128)(2,1)S(1)} %copy-done.30), channel_id=1, replica_groups=mesh['dp'=4,'ctx'=8] {'ctx'}, dimensions={0}, use_global_device_ids=true | all-gather | bytes 665856 | tf_op jit(solution)/shard_map/all_gather | solution.py:243
  157.3 14.6 %collective-permute-start.8 = (bf16[1088,272]{0,1:T(8,128)(2,1)}, bf16[1088,272]{0,1:T(8,128)(2,1)}, u32[]{:S(2)}, u32[]{:S(2)}) collective-permute-start(bf16[1088,272]{0,1:T(8,128)(2,1)} %copy.158), channel_id=1, source_target_pairs={{0,24},{8,0},{16,8},{24,16},{1,25},{9,1},{17,9},{25,17},{2,26},{10... | collective-permute-start | bytes 1775624 | tf_op jit(solution)/shard_map/ppermute | solution.py:159
  174.7 10.1 %all-gather.14.cloned.1.call-done = bf16[24,2,64,1152]{3,2,1,0:T(8,128)(2,1)} async-done(((bf16[3,2,64,1152]{3,2,1,0:T(8,128)(2,1)}), bf16[24,2,64,1152]{3,2,1,0:T(8,128)(2,1)}) %all-gather.14.cloned.1.call-update) | async-done | bytes 7077904 | tf_op jit(solution)/shard_map/all_gather | solution.py:274
  187.9 20.3 %shard_map.254 = (bf16[3,64,1152]{2,1,0:T(8,128)(2,1)S(1)}, bf16[3,18,64,512]{3,2,1,0:T(8,128)(2,1)S(1)}) custom-call(s32[3,64,1]{2,1,0:T(8,128)S(1)} %copy.157.first_ref, s32[3,64,1]{2,1,0:T(8,128)S(1)} %broadcast_in_dim.20.last_ref, bf16[3,64,1152]{2,1,0:T(8,128)(2,1)S(1)} %bitcast.225, bf16[8,3,2,64,1152]{4,3,2,1,0:T(8,128)(2,1)S(1)} %bitcast.213), custom_call_target="tpu_custom_call" | custom-call | tf_op jit(solution)/shard_map/pallas_call | solution.py:118
  234.7 8.0 %collective-permute-done.9 = bf16[192,1088]{1,0:T(8,128)(2,1)} collective-permute-done((bf16[192,1088]{1,0:T(8,128)(2,1)}, bf16[192,1088]{1,0:T(8,128)(2,1)}, u32[]{:S(2)}, u32[]{:S(2)}) %collective-permute-start.9) | collective-permute-done | bytes 417824 | tf_op jit(solution)/shard_map/ppermute | solution.py:159
  244.8 6.8 %collective-permute-done.10 = bf16[192,1088]{1,0:T(8,128)(2,1)} collective-permute-done((bf16[192,1088]{1,0:T(8,128)(2,1)}, bf16[192,1088]{1,0:T(8,128)(2,1)}, u32[]{:S(2)}, u32[]{:S(2)}) %collective-permute-start.10) | collective-permute-done | bytes 417824 | tf_op jit(solution)/shard_map/ppermute | solution.py:159
  255.7 6.8 %convolution_add_fusion = f32[768,1088]{0,1:T(8,128)} fusion(bf16[1088,1088]{1,0:T(8,128)(2,1)} %all-gather.10.cloned.1.call-done, f32[1088]{0:T(1024)} %convert_element_type.249, bf16[192,1088]{0,1:T(8,128)(2,1)} %copy.171, bf16[192,1088]{0,1:T(8,128)(2,1)} %copy.170, bf16[192,1088]{0,1:T(8,128)(2,1)} %copy.169, bf16[192,1088]{0,1:T(8,128)(2,1)} %get-tuple-element.132), kind=kOutput, calls=%fused_computation.10 | convolution fusion | flops 1825751040 | bytes 7385344 | tf_op jit(solution)/shard_map/dot_general | solution.py:183
  262.5 5.5 convolution_convert_fusion.7
  269.6 5.8 convert_reduce_fusion
  291.5 6.0 convolution_convert_fusion.1
  297.6 7.8 %collective-permute-done.19 = bf16[192,2176]{1,0:T(8,128)(2,1)} collective-permute-done((bf16[192,2176]{1,0:T(8,128)(2,1)}, bf16[192,2176]{1,0:T(8,128)(2,1)}, u32[]{:S(2)}, u32[]{:S(2)}) %collective-permute-start.19) | collective-permute-done | bytes 835616 | tf_op jit(solution)/shard_map/ppermute | solution.py:169
  307.7 18.2 %collective-permute-done.20 = bf16[192,2176]{1,0:T(8,128)(2,1)} collective-permute-done((bf16[192,2176]{1,0:T(8,128)(2,1)}, bf16[192,2176]{1,0:T(8,128)(2,1)}, u32[]{:S(2)}, u32[]{:S(2)}) %collective-permute-start.20) | collective-permute-done | bytes 835616 | tf_op jit(solution)/shard_map/ppermute | solution.py:169
  347.2 21.1 %shard_map.255 = (bf16[3,64,1152]{2,1,0:T(8,128)(2,1)S(1)}, bf16[8,3,2,64,1152]{4,3,2,1,0:T(8,128)(2,1)S(1)}) custom-call(bf16[3,64,1152]{2,1,0:T(8,128)(2,1)S(1)} %bitcast.226, bf16[8,3,2,64,1152]{4,3,2,1,0:T(8,128)(2,1)S(1)} %bitcast.216, bf16[3,64,1152]{2,1,0:T(8,128)(2,1)S(1)} %bitcast.230, bf16[3,18,64,512]{3,2,1,0:T(8,128)(2,1)S(1)} %copy-done.3), custom_call_target="tpu_custom_call" | custom-call | tf_op jit(solution)/shard_map/pallas_call | solution.py:134
  371.2 6.8 %convolution_convert_fusion = bf16[1088,1088]{1,0:T(8,128)(2,1)} fusion(bf16[192,1088]{1,0:T(8,128)(2,1)} %collective-permute-done.18, bf16[192,1088]{1,0:T(8,128)(2,1)} %collective-permute-done.17, bf16[192,1088]{1,0:T(8,128)(2,1)} %collective-permute-done.16, bf16[192,1088]{1,0:T(8,128)(2,1)S(1)} %bitcast.256, f32[768,1088]{0,1:T(8,128)} %convolution_add_fusion), kind=kOutput, calls=%fused_computation | convolution fusion | flops 1833619456 | bytes 7380992 | tf_op jit(solution)/shard_map/dot_general | solution.py:39
  387.3 11.9 %collective-permute-done.28 = bf16[1088,272]{0,1:T(8,128)(2,1)} collective-permute-done((bf16[1088,272]{0,1:T(8,128)(2,1)}, bf16[1088,272]{0,1:T(8,128)(2,1)}, u32[]{:S(2)}, u32[]{:S(2)}) %collective-permute-start.28) | collective-permute-done | bytes 591904 | tf_op jit(solution)/shard_map/ppermute | solution.py:169
  399.2 11.1 %collective-permute-done.29 = bf16[1088,272]{0,1:T(8,128)(2,1)} collective-permute-done((bf16[1088,272]{0,1:T(8,128)(2,1)}, bf16[1088,272]{0,1:T(8,128)(2,1)}, u32[]{:S(2)}, u32[]{:S(2)}) %collective-permute-start.29) | collective-permute-done | bytes 591904 | tf_op jit(solution)/shard_map/ppermute | solution.py:169
  415.5 33.1 %reduce-scatter.12.cloned.1.call-done = bf16[1,3,2,64,1152]{4,3,2,1,0:T(8,128)(2,1)} async-done(((bf16[8,3,2,64,1152]{4,3,2,1,0:T(8,128)(2,1)}), bf16[1,3,2,64,1152]{4,3,2,1,0:T(8,128)(2,1)}) %reduce-scatter.12.cloned.1.call-update) | async-done | bytes 884752 | tf_op jit(solution)/shard_map/reduce_scatter | solution.py:328
  489.6 49.3 %collective-permute-done.25 = f32[2176]{0:T(1024)S(1)} collective-permute-done((f32[2176]{0:T(1024)S(1)}, f32[2176]{0:T(1024)S(1)}, u32[]{:S(2)}, u32[]{:S(2)}) %collective-permute-start.25) | collective-permute-done | bytes 8736 | tf_op jit(solution)/shard_map/ppermute | solution.py:169
  556.6 8.3 %collective-permute-start.32 = (bf16[136,272]{1,0:T(8,128)(2,1)S(1)}, bf16[136,272]{1,0:T(8,128)(2,1)S(1)}, u32[]{:S(2)}, u32[]{:S(2)}) collective-permute-start(bf16[136,272]{1,0:T(8,128)(2,1)S(1)} %get-tuple-element.174), channel_id=1, source_target_pairs={{1,0},{5,1},{9,2},{13,3},{17,4},{21,5},{25,6},{29,7},{2,8},{6,9},{... | collective-permute-start | bytes 221960 | tf_op jit(solution)/shard_map/ppermute | solution.py:305
  569.7 23.4 %collective-permute-done.33 = bf16[136,272]{1,0:T(8,128)(2,1)S(1)} collective-permute-done((bf16[136,272]{1,0:T(8,128)(2,1)S(1)}, bf16[136,272]{1,0:T(8,128)(2,1)S(1)}, u32[]{:S(2)}, u32[]{:S(2)}) %collective-permute-start.33) | collective-permute-done | bytes 74016 | tf_op jit(solution)/shard_map/ppermute | solution.py:305
  (392 shorter events, 243.6 us)
Async XLA Ops:
  7.3 78.2 %all-gather.8.cloned.1.call-start = ((), (), s32[]{:S(2)}) async-start(), calls=%async_computation.5 | async-start | bytes 4386816 | tf_op jit(solution)/shard_map/all_gather | solution.py:241
  32.2 152.6 %all-gather.14.cloned.1.call-start = ((), (), s32[]{:S(2)}) async-start(), calls=%async_computation.10 | async-start | bytes 7962624 | tf_op jit(solution)/shard_map/all_gather | solution.py:274
  45.5 36.0 %collective-permute-start.4 = (bf16[1088,384]{1,0:T(8,128)(2,1)S(1)}, bf16[1088,384]{1,0:T(8,128)(2,1)}, u32[]{:S(2)}, u32[]{:S(2)}) collective-permute-start(bf16[1088,384]{1,0:T(8,128)(2,1)S(1)} %all_gather.29), channel_id=1, source_target_pairs={{0,16},{8,24},{16,0},{24,8},{1,17},{9,25},{17,1},{25,9},{2,18},{10... | collective-permute-start | bytes 2506760 | tf_op jit(solution)/shard_map/ppermute | solution.py:159
  46.3 37.5 %collective-permute-start.5 = (bf16[1088,384]{1,0:T(8,128)(2,1)S(1)}, bf16[1088,384]{1,0:T(8,128)(2,1)}, u32[]{:S(2)}, u32[]{:S(2)}) collective-permute-start(bf16[1088,384]{1,0:T(8,128)(2,1)S(1)} %all_gather.29), channel_id=1, source_target_pairs={{0,24},{8,0},{16,8},{24,16},{1,25},{9,1},{17,9},{25,17},{2,26},{10... | collective-permute-start | bytes 2506760 | tf_op jit(solution)/shard_map/ppermute | solution.py:159
  99.3 156.3 %all-gather.10.cloned.1.call-start = ((), (), s32[]{:S(2)}) async-start(), calls=%async_computation.6 | async-start | bytes 2820096 | tf_op jit(solution)/shard_map/all_gather | solution.py:245
  100.1 162.4 %all-gather.12.cloned.1.call-start = ((), (), s32[]{:S(2)}) async-start(), calls=%async_computation.7 | async-start | bytes 2820096 | tf_op jit(solution)/shard_map/all_gather | solution.py:256
  118.9 252.2 %reduce-scatter.16.cloned.1.call-start = ((), (), s32[]{:S(2)}) async-start(), calls=%async_computation.11 | async-start | bytes 2820096
  154.6 53.7 %collective-permute-start.6 = (bf16[1088,272]{0,1:T(8,128)(2,1)}, bf16[1088,272]{0,1:T(8,128)(2,1)}, u32[]{:S(2)}, u32[]{:S(2)}) collective-permute-start(bf16[1088,272]{0,1:T(8,128)(2,1)} %copy.158), channel_id=1, source_target_pairs={{0,8},{8,16},{16,24},{24,0},{1,9},{9,17},{17,25},{25,1},{2,10},{10... | collective-permute-start | bytes 1775624 | tf_op jit(solution)/shard_map/ppermute | solution.py:159
  155.4 54.8 %collective-permute-start.7 = (bf16[1088,272]{0,1:T(8,128)(2,1)}, bf16[1088,272]{0,1:T(8,128)(2,1)}, u32[]{:S(2)}, u32[]{:S(2)}) collective-permute-start(bf16[1088,272]{0,1:T(8,128)(2,1)} %copy.158), channel_id=1, source_target_pairs={{0,16},{8,24},{16,0},{24,8},{1,17},{9,25},{17,1},{25,9},{2,18},{10... | collective-permute-start | bytes 1775624 | tf_op jit(solution)/shard_map/ppermute | solution.py:159
  157.3 54.4 %collective-permute-start.8 = (bf16[1088,272]{0,1:T(8,128)(2,1)}, bf16[1088,272]{0,1:T(8,128)(2,1)}, u32[]{:S(2)}, u32[]{:S(2)}) collective-permute-start(bf16[1088,272]{0,1:T(8,128)(2,1)} %copy.158), channel_id=1, source_target_pairs={{0,24},{8,0},{16,8},{24,16},{1,25},{9,1},{17,9},{25,17},{2,26},{10... | collective-permute-start | bytes 1775624 | tf_op jit(solution)/shard_map/ppermute | solution.py:159
  231.4 36.6 %collective-permute-start.16 = (bf16[192,1088]{1,0:T(8,128)(2,1)S(1)}, bf16[192,1088]{1,0:T(8,128)(2,1)}, u32[]{:S(2)}, u32[]{:S(2)}) collective-permute-start(bf16[192,1088]{1,0:T(8,128)(2,1)S(1)} %bitcast.251), channel_id=1, source_target_pairs={{0,8},{8,16},{16,24},{24,0},{1,9},{9,17},{17,25},{25,1},{2,10},{10... | collective-permute-start | bytes 1253384 | tf_op jit(solution)/shard_map/ppermute | solution.py:159
  232.0 37.6 %collective-permute-start.17 = (bf16[192,1088]{1,0:T(8,128)(2,1)S(1)}, bf16[192,1088]{1,0:T(8,128)(2,1)}, u32[]{:S(2)}, u32[]{:S(2)}) collective-permute-start(bf16[192,1088]{1,0:T(8,128)(2,1)S(1)} %bitcast.252), channel_id=1, source_target_pairs={{0,16},{8,24},{16,0},{24,8},{1,17},{9,25},{17,1},{25,9},{2,18},{10... | collective-permute-start | bytes 1253384 | tf_op jit(solution)/shard_map/ppermute | solution.py:159
  288.3 37.6 %collective-permute-start.20 = (bf16[192,2176]{1,0:T(8,128)(2,1)}, bf16[192,2176]{1,0:T(8,128)(2,1)}, u32[]{:S(2)}, u32[]{:S(2)}) collective-permute-start(bf16[192,2176]{1,0:T(8,128)(2,1)} %copy.175), channel_id=1, source_target_pairs={{0,16},{8,24},{16,0},{24,8},{1,17},{9,25},{17,1},{25,9},{2,18},{10... | collective-permute-start | bytes 2506760 | tf_op jit(solution)/shard_map/ppermute | solution.py:169
  290.9 37.3 %collective-permute-start.21 = (bf16[192,2176]{1,0:T(8,128)(2,1)}, bf16[192,2176]{1,0:T(8,128)(2,1)}, u32[]{:S(2)}, u32[]{:S(2)}) collective-permute-start(bf16[192,2176]{1,0:T(8,128)(2,1)} %copy.177), channel_id=1, source_target_pairs={{0,8},{8,16},{16,24},{24,0},{1,9},{9,17},{17,25},{25,1},{2,10},{10... | collective-permute-start | bytes 2506760 | tf_op jit(solution)/shard_map/ppermute | solution.py:169
  334.7 114.0 %reduce-scatter.12.cloned.1.call-start = ((), (), s32[]{:S(2)}) async-start(), calls=%async_computation.8 | async-start | bytes 7962624 | tf_op jit(solution)/shard_map/reduce_scatter | solution.py:328
  371.2 183.4 %reduce-scatter.20.cloned.1.call-start = ((), (), s32[]{:S(2)}) async-start(), calls=%async_computation.13 | async-start | bytes 2820096
  378.1 190.0 %reduce-scatter.18.cloned.1.call-start = ((), (), s32[]{:S(2)}) async-start(), calls=%async_computation.12 | async-start | bytes 940032
  415.5 194.8 %reduce-scatter.14.cloned.1.call-start = ((), (), s32[]{:S(2)}) async-start(), calls=%async_computation.9 | async-start | bytes 2322432 | tf_op jit(solution)/shard_map/reduce_scatter | solution.py:367
  457.5 86.6 %collective-permute-start.22 = (bf16[1088,816]{0,1:T(8,128)(2,1)}, bf16[1088,816]{0,1:T(8,128)(2,1)}, u32[]{:S(2)}, u32[]{:S(2)}) collective-permute-start(bf16[1088,816]{0,1:T(8,128)(2,1)} %convolution_convert_fusion.4), channel_id=1, source_target_pairs={{0,24},{8,0},{16,8},{24,16},{1,25},{9,1},{17,9},{25,17},{2,26},{10... | collective-permute-start | bytes 5326856 | tf_op jit(solution)/shard_map/ppermute | solution.py:169
  462.0 82.2 %collective-permute-start.23 = (bf16[1088,816]{0,1:T(8,128)(2,1)}, bf16[1088,816]{0,1:T(8,128)(2,1)}, u32[]{:S(2)}, u32[]{:S(2)}) collective-permute-start(bf16[1088,816]{0,1:T(8,128)(2,1)} %convolution_convert_fusion.3), channel_id=1, source_target_pairs={{0,16},{8,24},{16,0},{24,8},{1,17},{9,25},{17,1},{25,9},{2,18},{10... | collective-permute-start | bytes 5326856 | tf_op jit(solution)/shard_map/ppermute | solution.py:169
  464.5 79.7 %collective-permute-start.24 = (bf16[1088,816]{0,1:T(8,128)(2,1)}, bf16[1088,816]{0,1:T(8,128)(2,1)}, u32[]{:S(2)}, u32[]{:S(2)}) collective-permute-start(bf16[1088,816]{0,1:T(8,128)(2,1)} %convolution_convert_fusion.2), channel_id=1, source_target_pairs={{0,8},{8,16},{16,24},{24,0},{1,9},{9,17},{17,25},{25,1},{2,10},{10... | collective-permute-start | bytes 5326856 | tf_op jit(solution)/shard_map/ppermute | solution.py:169
  485.7 53.2 %collective-permute-start.25 = (f32[2176]{0:T(1024)S(1)}, f32[2176]{0:T(1024)S(1)}, u32[]{:S(2)}, u32[]{:S(2)}) collective-permute-start(f32[2176]{0:T(1024)S(1)} %get-tuple-element.126), channel_id=1, source_target_pairs={{0,24},{8,0},{16,8},{24,16},{1,25},{9,1},{17,9},{25,17},{2,26},{10... | collective-permute-start | bytes 26120 | tf_op jit(solution)/shard_map/ppermute | solution.py:169
  488.1 55.0 %collective-permute-start.26 = (f32[2176]{0:T(1024)S(1)}, f32[2176]{0:T(1024)S(1)}, u32[]{:S(2)}, u32[]{:S(2)}) collective-permute-start(f32[2176]{0:T(1024)S(1)} %get-tuple-element.128), channel_id=1, source_target_pairs={{0,16},{8,24},{16,0},{24,8},{1,17},{9,25},{17,1},{25,9},{2,18},{10... | collective-permute-start | bytes 26120 | tf_op jit(solution)/shard_map/ppermute | solution.py:169
  565.0 32.6 %collective-permute-start.34 = (bf16[136,272]{1,0:T(8,128)(2,1)S(1)}, bf16[136,272]{1,0:T(8,128)(2,1)S(1)}, u32[]{:S(2)}, u32[]{:S(2)}) collective-permute-start(bf16[136,272]{1,0:T(8,128)(2,1)S(1)} %get-tuple-element.172), channel_id=1, source_target_pairs={{3,0},{7,1},{11,2},{15,3},{19,4},{23,5},{27,6},{31,7},{0,8},{4,9},... | collective-permute-start | bytes 221960 | tf_op jit(solution)/shard_map/ppermute | solution.py:305
  (89 other events, 1389.3 us)
Sparse Core Ops, SparseCore 0:
  32.3 43.9 all-gather.7
  99.5 85.3 all-gather.13
  186.5 30.0 all-gather.9
  218.6 31.9 all-gather.11
  334.8 35.4 reduce-scatter.15
  372.6 75.9 reduce-scatter.11
  451.0 36.5 reduce-scatter.19
  490.0 31.2 reduce-scatter.17
  553.9 55.0 reduce-scatter.13
